TPU v7x, 32 devices: a whole 2x2x4 slice. The times are simulated.
32 devices in a mesh: orb: 2 (over y), aux: 16 (over z, x, core).
Axes of the slice: x: 2, y: 2, z: 4, core: 2. Of those that a mesh axis runs over, the one named last changes fastest.
Arguments:
- factors: bfloat16 [4, 32768, 512], P('orb', 'aux'), may hold values from -0.5 to 0.5
- occ_energy: float32 [4], replicated, may hold values from -2 to -0.5
- virt_energy: float32 [4, 512], replicated, may hold values from 0.2 to 3
- tile_table: int32 [4, 3], replicated, may hold values from 0 to 3, as said below
Outputs:
- gamma: bfloat16 [4, 32768, 512], P('orb', 'aux')
Inputs may be any that keep to these rules, and one draw needn't show every extreme that they name: Row t names two different blocks and the group tile_table[t, 2] that computes the tile. Each group computes at most 4 tiles, and some group exactly 4. Of the blocks owned by another group, the tiles of one group name at most one.
All inputs are finite; a program needn't handle non-finite values.
Results may differ from a plain program's by a relative error of at most 0.0053.
Values may be sent and summed in bfloat16 or wider, within the bound.
No kernel may reach another device: no remote copies, remote signals or barrier semaphores. Data moves between devices by JAX's collectives and lax.ppermute only.
A program may use at most 192 MiB of HBM per device.

v0:
```python
import functools

import jax
import jax.numpy as jnp
from jax import lax
from jax.experimental import pallas as pl
from jax.experimental.pallas import tpu as pltpu
from jax.sharding import PartitionSpec as P

CAP = 4
WIRE = jnp.bfloat16
HELPS, FOREIGN, PLACE, COUNTS, LOW, PARTNER = 0, 1, 2, 3, 6, 7
MEBI = 1024 * 1024
SMEM_SPEC = pl.BlockSpec(memory_space=pltpu.SMEM)
HBM_SPEC = pl.BlockSpec(memory_space=pltpu.HBM)
VMEM_SPEC = pl.BlockSpec(memory_space=pltpu.VMEM)


def general(factors, occ_energy, virt_energy, tile_table):
    owned = factors.shape[0]
    width = factors.shape[2]
    tiles = tile_table.shape[0]
    groups = lax.axis_size("orb")
    mine = lax.axis_index("orb")
    first = tile_table[:, 0]
    second = tile_table[:, 1]
    helper = tile_table[:, 2]
    block_ids = jnp.arange(owned * groups, dtype=jnp.int32)
    group_ids = jnp.arange(groups, dtype=jnp.int32)
    local_ids = jnp.arange(owned, dtype=jnp.int32)
    touched = (
        (first[:, None] == block_ids[None, :]) | (second[:, None] == block_ids[None, :])
    ).astype(jnp.int32)
    helped = (helper[:, None] == group_ids[None, :]).astype(jnp.int32)
    usage = jnp.sum(helped[:, :, None] * touched[:, None, :], axis=0) > 0
    usage = usage.reshape(groups, groups, owned).astype(jnp.int32)
    own_usage = jnp.take(usage, mine, axis=1)
    send_pick = jnp.sum(own_usage * local_ids[None, :], axis=1)
    outgoing = jnp.stack(
        [
            lax.dynamic_index_in_dim(factors, send_pick[group], 0, keepdims=False)
            for group in range(groups)
        ]
    )
    incoming = lax.all_to_all(outgoing, "orb", split_axis=0, concat_axis=0, tiled=True)
    store = jnp.concatenate([factors, incoming], axis=0)

    def position(block):
        owner = block // owned
        return jnp.where(owner == mine, block % owned, owned + owner)

    is_mine = (helper == mine).astype(jnp.int32)
    tile_ids = jnp.arange(tiles, dtype=jnp.int32)
    earlier = (tile_ids[None, :] < tile_ids[:, None]).astype(jnp.int32)
    rank = jnp.sum(earlier * is_mine[None, :], axis=1)
    slot_ids = jnp.arange(CAP, dtype=jnp.int32)
    picked = is_mine[None, :] * (rank[None, :] == slot_ids[:, None]).astype(jnp.int32)
    valid = jnp.sum(picked, axis=1)
    tile_p = jnp.sum(picked * first[None, :], axis=1)
    tile_q = jnp.sum(picked * second[None, :], axis=1)
    place_p = position(tile_p)
    place_q = position(tile_q)
    energy_p = jnp.take(virt_energy, tile_p, axis=0)
    energy_q = jnp.take(virt_energy, tile_q, axis=0)
    occ_sum = jnp.take(occ_energy, tile_p) + jnp.take(occ_energy, tile_q)
    denominators = energy_p[:, :, None] + energy_q[:, None, :] - occ_sum[:, None, None]

    def partners(slot):
        block_p = lax.dynamic_index_in_dim(store, place_p[slot], 0, keepdims=False)
        block_q = lax.dynamic_index_in_dim(store, place_q[slot], 0, keepdims=False)
        return (block_p, block_q)

    def fill(slot, buffer):
        block_p, block_q = partners(slot)
        return lax.dynamic_update_index_in_dim(buffer, outer(block_p, block_q), slot, 0)

    buffer = lax.fori_loop(0, CAP, fill, jnp.zeros((CAP, width, width), jnp.float32))
    summed = lax.psum(buffer, "aux")
    all_amps = (summed / denominators).astype(jnp.bfloat16)

    def apply_all(slot, gathered):
        block_p, block_q = partners(slot)
        amplitudes = lax.dynamic_index_in_dim(all_amps, slot, 0, keepdims=False)
        amplitudes = jnp.where(valid[slot] > 0, amplitudes, jnp.zeros_like(amplitudes))
        gathered = gathered.at[place_p[slot]].add(right_t(block_q, amplitudes))
        return gathered.at[place_q[slot]].add(right(block_p, amplitudes))

    gathered = lax.fori_loop(0, CAP, apply_all, jnp.zeros(store.shape, jnp.float32))
    helper_part = gathered[owned:].astype(jnp.bfloat16)
    returned = lax.all_to_all(helper_part, "orb", split_axis=0, concat_axis=0, tiled=True)
    landing = (send_pick[:, None] == local_ids[None, :]).astype(jnp.float32)
    gamma = gathered[:owned] + jnp.einsum(
        "dj,dav->jav", landing, returned.astype(jnp.float32), precision=lax.Precision.HIGHEST
    )
    return gamma.astype(jnp.bfloat16)


def outer(a, b):
    return lax.dot_general(a, b, (((0,), (0,)), ((), ())), preferred_element_type=jnp.float32)


def right(a, m):
    return jnp.dot(a, m, preferred_element_type=jnp.float32)


def right_t(a, m):
    return lax.dot_general(a, m, (((1,), (1,)), ((), ())), preferred_element_type=jnp.float32)


def swap(value, axis, bit):
    size = lax.axis_size(axis)
    return lax.ppermute(value, axis, [(i, i ^ (1 << bit)) for i in range(size)])


def direct(value, bits, e):
    mask = sum(1 << (bits - 1 - n) for n in range(bits - 1) if (e >> n) & 1)
    size = 1 << bits
    return lax.ppermute(value, "aux", [(i, i ^ mask) for i in range(size)])


def gather(part, bits):
    near = jnp.concatenate([part, direct(part, bits, 1 << (bits - 2))], axis=0)
    return near, swap(near, "aux", 0)


def gather_lower(part, bits):
    upper = 1 << (bits - 2)
    pieces = [part[None]] + [direct(part, bits, e)[None] for e in range(1, upper)]
    while len(pieces) > 1:
        pieces = [jnp.concatenate(pieces[n : n + 2], axis=0) for n in range(0, len(pieces), 2)]
    return pieces[0]


def join_kernel(shift, plan, kept, came, own, *others):
    _, size, _ = own.shape
    count = 1 + len(others)
    place = (plan[PLACE] >> shift) & (count - 1)
    for e, out in enumerate((own, *others)):
        rows = pl.ds(pl.multiple_of((place ^ e) * size, size), size)
        total = kept[:, rows, :] + came[:, rows, :].astype(jnp.float32)
        out[...] = total.astype(out.dtype)


def after(value, *others):
    return lax.optimization_barrier((value, *others))[0]


def start_all(copies):
    for copy in copies:
        copy.start()


def wait_all(copies):
    for copy in copies:
        copy.wait()


def staged(source, stage, target, sems):
    first = pltpu.make_async_copy(source, stage, sems.at[0])
    return first, pltpu.make_async_copy(stage, target, sems.at[1])


def relay(copies):
    for first, second in copies:
        first.wait()
        second.start()


def rows_at(unit, start, size):
    return pl.ds(pl.multiple_of(start * unit, unit), size * unit)


def plan_kernel(tiles, bits, step, table, factors, plan, pay, stage, sems):
    helper = table[0, 2]
    helps = (lax.axis_index("orb") == helper).astype(jnp.int32)
    low, foreign_low = helper * 2, (1 - helper) * 2
    foreign = jnp.int32(0)
    for t in range(tiles):
        named = (table[t, 0] == foreign_low + 1) | (table[t, 1] == foreign_low + 1)
        foreign = foreign | named.astype(jnp.int32)
    b0, b1 = jnp.where(helps == 1, 0, foreign), jnp.where(helps == 1, 1, foreign)
    sources = ((b0, 2 * helps), (b0, 2 * helps + 1), (b1, 2 + helps))
    copies = [
        staged(
            factors.at[block, rows_at(step, start, 1)],
            stage.at[pl.ds(n * step, step)],
            pay.at[pl.ds(n * step, step)],
            sems.at[n],
        )
        for n, (block, start) in enumerate(sources)
    ]
    start_all(first for first, _ in copies)
    me = lax.axis_index("aux")
    place = jnp.int32(0)
    for bit in range(bits):
        place = place * 2 + ((me >> bit) & 1)
    plan[HELPS], plan[FOREIGN], plan[PLACE] = helps, foreign, place
    plan[LOW], plan[PARTNER] = low, foreign_low + foreign
    pairs = ((low, low + 1), (low, foreign_low + foreign), (low + 1, foreign_low + foreign))
    for n, (a, b) in enumerate(pairs):
        count = jnp.int32(0)
        for t in range(tiles):
            p, q = table[t, 0], table[t, 1]
            same = ((p == a) & (q == b)) | ((p == b) & (q == a))
            count = count + same.astype(jnp.int32)
        plan[COUNTS + n] = count
    relay(copies)
    wait_all(second for _, second in copies)


def weigh_kernel(step, plan, occ, virt, factors, own_weight, weights, pay_a, stage, sems):
    helps, foreign = plan[HELPS], plan[FOREIGN]
    b0, b1 = jnp.where(helps == 1, 0, foreign), jnp.where(helps == 1, 1, foreign)
    copies = [
        staged(
            factors.at[block, rows_at(step, start, 1)],
            stage.at[pl.ds(n * step, step)],
            pay_a.at[pl.ds(n * step, step)],
            sems.at[n],
        )
        for n, (block, start) in enumerate(((b1, 3 - helps), (b0, 1)))
    ]
    start_all(first for first, _ in copies)
    low, partner = plan[LOW], plan[PARTNER]
    _, shard, width = own_weight.shape
    row = lax.broadcasted_iota(jnp.int32, (shard, width), 0)
    column = lax.broadcasted_iota(jnp.int32, (shard, width), 1)
    mine = column == row + plan[PLACE] * shard
    pairs = ((low, low + 1, own_weight, 0), (low, partner, weights, 0), (low + 1, partner, weights, 1))
    for n, (a, b, out, slot) in enumerate(pairs):
        virt_a = jnp.sum(jnp.where(mine, virt[pl.ds(a, 1), :], 0.0), axis=1, keepdims=True)
        denominators = virt_a + virt[pl.ds(b, 1), :] - occ[a] - occ[b]
        out[slot] = plan[COUNTS + n].astype(jnp.float32) / denominators
    relay(copies)
    wait_all(second for _, second in copies)


def third_rows(unit, plan, factors, pay_b, stage, sems):
    helps, foreign = plan[HELPS], plan[FOREIGN]
    b0, b1 = jnp.where(helps == 1, 0, foreign), jnp.where(helps == 1, 1, foreign)
    return [
        staged(
            factors.at[block, pl.ds(start * unit, size * unit)],
            stage.at[pl.ds(to * unit, size * unit)],
            pay_b.at[pl.ds(to * unit, size * unit)],
            sems.at[n],
        )
        for n, (block, start, size, to) in enumerate(((b1, 2, 2, 0), (b0, 1, 1, 2), (b1, 1, 1, 3)))
    ]


def pack_kernel(unit, plan, factors, pay_b, stage, sems):
    copies = third_rows(unit, plan, factors, pay_b, stage, sems)
    start_all(first for first, _ in copies)
    relay(copies)
    wait_all(second for _, second in copies)


def split_halves(acc, pair, kept, sent, core):
    half = kept.shape[1]
    kept[pair] = acc[pl.ds(pl.multiple_of(core * half, half), half), :]
    other = acc[pl.ds(pl.multiple_of((1 - core) * half, half), half), :]
    sent[pair] = other.astype(sent.dtype)


def own_kernel(step, plan, factors, kept, sent, rows, acc, sems):
    del plan
    copies = [
        pltpu.make_async_copy(
            factors.at[:, pl.ds(n * step, step)], rows.at[:, pl.ds(n * step, step)], sems.at[n]
        )
        for n in range(4)
    ]
    start_all(copies)
    for n in range(4):
        copies[n].wait()
        term = outer(rows[0, n * step : (n + 1) * step], rows[1, n * step : (n + 1) * step])
        acc[...] = term if n == 0 else acc[...] + term
    split_halves(acc, 0, kept, sent, lax.axis_index("aux") & 1)


def pair_kernel(
    step, plan, factors, got_hbm, kept, sent, pay_b, got, rows0, rows1, acc0, acc1, stage, sems, pay_sems
):
    helps, foreign = plan[HELPS], plan[FOREIGN]
    b0, b1 = jnp.where(helps == 1, 0, foreign), jnp.where(helps == 1, 1, foreign)

    def cut(ref, n):
        return ref[n * step : (n + 1) * step]

    def fetch(source, ref, n, slot):
        return pltpu.make_async_copy(source, ref.at[pl.ds(n * step, step)], sems.at[slot])

    gots = [fetch(got_hbm.at[pl.ds(n * step, step)], got, n, n) for n in range(3)]
    copies0 = [
        fetch(factors.at[b0, rows_at(step, jnp.where(helps == 1, n, 2 + n), 1)], rows0, n, 3 + n)
        for n in range(2)
    ]
    copies1 = [
        fetch(factors.at[b1, rows_at(step, jnp.where(helps == 1, n, 3), 1)], rows1, n, 5 + n)
        for n in range(3)
    ]
    start_all((gots[0], copies0[0], gots[1], copies0[1], gots[2], copies1[2], *copies1[:2]))
    pays = third_rows(step // 2, plan, factors, pay_b, stage, pay_sems)
    start_all(first for first, _ in pays)

    for n in range(2):
        wait_all((gots[n], copies0[n]))

        @pl.when(helps == 1)
        def _():
            term = outer(cut(rows0, n), cut(got, n))
            acc0[...] = term if n == 0 else acc0[...] + term

        @pl.when(helps == 0)
        def _():
            term = outer(cut(got, n), cut(rows0, n))
            acc0[...] = term if n == 0 else acc0[...] + term

    wait_all((gots[2], copies1[2]))

    @pl.when(helps == 1)
    def _():
        acc1[...] = outer(cut(rows1, 2), cut(got, 2))

    @pl.when(helps == 0)
    def _():
        acc1[...] = outer(cut(got, 2), cut(rows1, 2))

    wait_all(copies1[:2])
    relay(pays)

    @pl.when(helps == 1)
    def _():
        acc1[...] += outer(cut(rows1, 0), cut(got, 0)) + outer(cut(rows1, 1), cut(got, 1))

    core = lax.axis_index("aux") & 1
    split_halves(acc0, 0, kept, sent, core)
    split_halves(acc1, 1, kept, sent, core)
    wait_all(second for _, second in pays)


def arrange(plan, near, far, pair, out):
    count, _, shard, _ = near.shape
    for source, base in ((near, 0), (far, count)):
        for n in range(count):
            row = pl.multiple_of((plan[PLACE] ^ (base + n)) * shard, shard)
            out[pl.ds(row, shard), :] = source[n, pair]


def back_kernel(plan, near_hbm, far_hbm, factors, back, amp0, amp1, wide, rows, sems):
    unit = back.shape[0]
    copies = [
        pltpu.make_async_copy(near_hbm, wide.at[0], sems.at[0]),
        pltpu.make_async_copy(far_hbm, wide.at[1], sems.at[1]),
        pltpu.make_async_copy(factors.at[:, pl.ds(0, unit)], rows, sems.at[2]),
    ]
    start_all(copies)
    wait_all(copies)
    arrange(plan, wide.at[0], wide.at[1], 0, amp0)
    arrange(plan, wide.at[0], wide.at[1], 1, amp1)
    total = right(rows[0], amp0[...]) + right(rows[1], amp1[...])
    back[...] = total.astype(back.dtype)


def last_kernel(
    step, plan, near01, far01, amp0, amp1, got1, got_a, got_b, factors, gamma, small, rows, own, out, own_amp, ins, outs
):
    unit = step // 2
    foreign = plan[FOREIGN]

    def part(start, size):
        return pl.ds(start * unit, size * unit)

    def copy(source, target, slot):
        return pltpu.make_async_copy(source, target, ins.at[slot])

    @pl.when(plan[HELPS] == 1)
    def _():
        singles = [copy(near01, small.at[0], 2), copy(far01, small.at[1], 3)]
        sources = [got1.at[part(2 * n, 2)] for n in range(3)] + [got_a.at[part(0, 2)]]
        others = [copy(sources[n], rows.at[part(2 * n, 2)], 4 + n) for n in range(4)]
        mine = [copy(factors.at[:, part(2 * n, 2)], own.at[:, part(2 * n, 2)], 8 + n) for n in range(4)]
        start_all(singles)
        for n in range(4):
            start_all((mine[n], others[n]))
        wait_all(singles)
        arrange(plan, small.at[0], small.at[1], 0, own_amp)
        results = []
        for n in range(4):
            wait_all((mine[n], others[n]))
            at = slice(n * step, (n + 1) * step)
            first = right_t(own[1, at], own_amp[...]) + right_t(rows[at], amp0[...])
            out[0, at] = first.astype(out.dtype)
            second = right(own[0, at], own_amp[...]) + right_t(rows[at], amp1[...])
            out[1, at] = second.astype(out.dtype)
            place = part(2 * n, 2)
            results.append(pltpu.make_async_copy(out.at[:, place], gamma.at[:, place], outs.at[n]))
            results[-1].start()
        wait_all(results)

    @pl.when(plan[HELPS] == 0)
    def _():
        others = [
            copy(got1, rows.at[part(0, 6)], 4),
            copy(got_a, rows.at[part(6, 4)], 5),
            copy(got_b, rows.at[part(10, 4)], 6),
        ]
        start_all(others)
        out[0] = jnp.zeros_like(out[0])
        results = [pltpu.make_async_copy(out.at[0], gamma.at[1 - foreign], outs.at[0])]
        results[0].start()
        wait_all(others)
        pieces = ((6, 2, 2, 4), (4, 2, 0, 6), (2, 2, 8, 10), (1, 1, 12, 13))
        for n, (start, size, row0, row1) in enumerate(pieces):
            rows0 = rows[row0 * unit : (row0 + size) * unit]
            rows1 = rows[row1 * unit : (row1 + size) * unit]
            total = right(rows0, amp0[...]) + right(rows1, amp1[...])
            out[1, start * unit : (start + size) * unit] = total.astype(out.dtype)
            place = part(start, size)
            results.append(
                pltpu.make_async_copy(out.at[1, place], gamma.at[foreign, place], outs.at[1 + n])
            )
            results[-1].start()
        wait_all(results)


def put_kernel(unit, plan, back, gamma_in, gamma, sem):
    @pl.when(plan[HELPS] == 0)
    def _():
        copy = pltpu.make_async_copy(back, gamma.at[plan[FOREIGN], pl.ds(0, unit)], sem)
        copy.start()
        copy.wait()


def two_groups(factors, occ_energy, virt_energy, tile_table):
    owned, rows, width = factors.shape
    aux = lax.axis_size("aux")
    bits = aux.bit_length() - 1
    step, unit = rows // 4, rows // 8
    shard = width // aux
    dtype = factors.dtype
    dma = pltpu.SemaphoreType.DMA

    def array(*shape, dtype=dtype):
        return jax.ShapeDtypeStruct(shape, dtype)

    def call(kernel, out_shape, in_specs, out_specs, scratch, cost=0, mebi=16, **options):
        return pl.pallas_call(
            kernel,
            out_shape=out_shape,
            in_specs=in_specs,
            out_specs=out_specs,
            scratch_shapes=scratch,
            compiler_params=pltpu.CompilerParams(vmem_limit_bytes=mebi * MEBI),
            cost_estimate=pl.CostEstimate(
                flops=cost * 2 * step * width * width,
                bytes_accessed=2 * step * width * 2,
                transcendentals=0,
            ),
            **options,
        )

    plan, pay1 = call(
        functools.partial(plan_kernel, tile_table.shape[0], bits, step),
        (array(8, dtype=jnp.int32), array(3 * step, width)),
        [SMEM_SPEC, HBM_SPEC],
        (SMEM_SPEC, HBM_SPEC),
        [pltpu.VMEM((3 * step, width), dtype), dma((3, 2))],
        mebi=61,
    )(tile_table, factors)
    got1 = swap(pay1, "orb", 0)

    def halves(pairs):
        kept = array(pairs, width // 2, width, dtype=jnp.float32)
        return kept, array(pairs, width // 2, width, dtype=WIRE)

    square = pltpu.VMEM((width, width), jnp.float32)

    def scatter(kept, sent):
        upper = aux // 4

        def join(kept, came, shift, count):
            shape = (kept.shape[0], kept.shape[1] // count, width)
            return call(
                functools.partial(join_kernel, shift),
                (array(*shape, dtype=jnp.float32), *[array(*shape, dtype=WIRE)] * (count - 1)),
                [SMEM_SPEC, VMEM_SPEC, VMEM_SPEC],
                (VMEM_SPEC,) * count,
                [],
            )(plan, kept, came)

        kept, sent = join(kept, swap(sent, "aux", 0), bits - 2, 2)
        own, *sends = join(kept, direct(sent, bits, upper), 0, upper)
        for term in [direct(send, bits, 1 + n) for n, send in enumerate(sends)]:
            own = own + term.astype(jnp.float32)
        return own

    def prepare():
        return call(
            functools.partial(weigh_kernel, step),
            (
                array(1, shard, width, dtype=jnp.float32),
                array(2, shard, width, dtype=jnp.float32),
                array(2 * step, width),
            ),
            [SMEM_SPEC, SMEM_SPEC, VMEM_SPEC, HBM_SPEC],
            (VMEM_SPEC, VMEM_SPEC, HBM_SPEC),
            [pltpu.VMEM((2 * step, width), dtype), dma((2, 2))],
        )(plan, occ_energy, virt_energy, factors)

    def own_chain():
        kept, sent = call(
            functools.partial(own_kernel, step),
            halves(1),
            [SMEM_SPEC, HBM_SPEC],
            (VMEM_SPEC, VMEM_SPEC),
            [pltpu.VMEM(factors.shape, dtype), square, dma((4,))],
            4,
        )(plan, factors)
        own_weight, weights, pay_a = prepare()
        shards01 = (scatter(kept, sent) * own_weight).astype(dtype)
        return gather_lower(shards01, bits), weights, pay_a

    def no_chain():
        return jnp.zeros((aux // 4, 1, shard, width), dtype), *prepare()[1:]

    part01, weights, pay_a = lax.cond(plan[COUNTS] > 0, own_chain, no_chain)
    used = plan[COUNTS + 1] + plan[COUNTS + 2] > 0
    got1, part01, weights, pay_a, used = lax.optimization_barrier(
        (got1, part01, weights, pay_a, used)
    )
    got_a = swap(pay_a, "orb", 0)

    def pair_chain():
        kept, sent, pay_b = call(
            functools.partial(pair_kernel, step),
            (*halves(2), array(4 * unit, width)),
            [SMEM_SPEC, HBM_SPEC, HBM_SPEC],
            (VMEM_SPEC, VMEM_SPEC, HBM_SPEC),
            [
                pltpu.VMEM((3 * step, width), dtype),
                pltpu.VMEM((2 * step, width), dtype),
                pltpu.VMEM((3 * step, width), dtype),
                square,
                square,
                pltpu.VMEM((4 * unit, width), dtype),
                dma((8,)),
                dma((3, 2)),
            ],
            5,
        )(plan, factors, got1)
        return scatter(kept, sent), pay_b, *gather(part01, bits)

    def no_pairs():
        pay_b = call(
            functools.partial(pack_kernel, unit),
            array(4 * unit, width),
            [SMEM_SPEC, HBM_SPEC],
            HBM_SPEC,
            [pltpu.VMEM((4 * unit, width), dtype), dma((3, 2))],
        )(plan, factors)
        return jnp.zeros((2, shard, width), jnp.float32), pay_b, *gather(part01, bits)

    sums, pay_b, near01, far01 = lax.cond(used, pair_chain, no_pairs)
    sums, got_a, pay_b = lax.optimization_barrier((sums, got_a, pay_b))
    sums = sums + swap(sums.astype(WIRE), "orb", 0).astype(jnp.float32)
    shards0, pay_b = lax.optimization_barrier(((sums * weights).astype(dtype), pay_b))
    got_b = swap(pay_b, "orb", 0)

    def nothing():
        half = jnp.zeros((aux // 2, 2, shard, width), dtype)
        return half, half

    near, far = lax.cond(used, lambda: gather(gather_lower(shards0, bits), bits), nothing)

    amp = array(width, width)
    back, amp0, amp1 = call(
        back_kernel,
        (array(unit, width), amp, amp),
        [SMEM_SPEC] + [HBM_SPEC] * 3,
        (VMEM_SPEC,) * 3,
        [
            pltpu.VMEM((2, *near.shape), dtype),
            pltpu.VMEM((2, unit, width), dtype),
            dma((3,)),
        ],
        1,
    )(plan, near, far, factors)
    got_back = swap(back, "orb", 0)

    gamma = call(
        functools.partial(last_kernel, step),
        array(*factors.shape),
        [SMEM_SPEC] + [HBM_SPEC] * 2 + [VMEM_SPEC] * 2 + [HBM_SPEC] * 4,
        HBM_SPEC,
        [
            pltpu.VMEM((2, *near01.shape), dtype),
            pltpu.VMEM((14 * unit, width), dtype),
            pltpu.VMEM(factors.shape, dtype),
            pltpu.VMEM(factors.shape, dtype),
            pltpu.VMEM((width, width), dtype),
            dma((12,)),
            dma((5,)),
        ],
        12,
        mebi=32,
    )(plan, near01, far01, amp0, amp1, got1, got_a, got_b, factors)
    return call(
        functools.partial(put_kernel, unit),
        array(*factors.shape),
        [SMEM_SPEC, VMEM_SPEC, HBM_SPEC],
        HBM_SPEC,
        [dma],
        input_output_aliases={2: 0},
    )(plan, got_back, gamma)


def shards(factors, occ_energy, virt_energy, tile_table):
    groups = lax.axis_size("orb")
    aux = lax.axis_size("aux")
    simple = groups == 2 and factors.shape[0] == 2 and tile_table.shape[0] <= CAP
    width = factors.shape[2]
    whole_shards = aux >= 4 and aux & (aux - 1) == 0 and width % (32 * aux) == 0
    if simple and whole_shards and factors.shape[1] % 128 == 0:
        return two_groups(factors, occ_energy, virt_energy, tile_table)
    return general(factors, occ_energy, virt_energy, tile_table)


def solution(mesh):
    return jax.shard_map(
        shards,
        mesh=mesh,
        in_specs=(P("orb", "aux", None), P(), P(), P()),
        out_specs=P("orb", "aux", None),
        check_vma=False,
    )
```

profile of v0, /device:TPU:0, one launch (start us, length us, event | category | flops | bytes accessed | tf_op | source)
XLA Modules:
  0.0 105.0 jit_solution(4962640484563280950)
XLA Ops:
  0.0 3.7 %shard_map.46 = (s32[8]{0:T(128)S(1)}, bf16[1536,512]{1,0:T(8,128)(2,1)}) custom-call(s32[4,3]{1,0:T(4,128)} %table.1, bf16[2,2048,512]{2,1,0:T(8,128)(2,1)} %factors.5), custom_call_target="tpu_custom_call" | custom-call | bytes 1048576 | tf_op jit(solution)/shard_map/pallas_call | solution.py:464
  3.7 3.0 %collective-permute-start.22 = (bf16[1536,512]{1,0:T(8,128)(2,1)}, bf16[1536,512]{1,0:T(8,128)(2,1)}, u32[]{:S(2)}, u32[]{:S(2)}) collective-permute-start(bf16[1536,512]{1,0:T(8,128)(2,1)} %get-tuple-element.98), channel_id=1, source_target_pairs={{0,16},{16,0},{1,17},{17,1},{2,18},{18,2},{3,19},{19,3},{4,20},{20... | collective-permute-start | bytes 4718600 | tf_op jit(solution)/shard_map/ppermute | solution.py:112
  9.3 28.5 %conditional.3 = (bf16[4,1,32,512]{3,2,1,0:T(8,128)(2,1)S(1)}, f32[2,32,512]{2,1,0:T(8,128)S(1)}, bf16[1024,512]{1,0:T(8,128)(2,1)}) conditional(s32[]{:T(128)} %bitcast.8, (s32[8]{0:T(128)S(1)}, f32[4]{0:T(128)S(1)}, f32[4,512]{1,0:T(4,128)S(1)}, bf16[2,2048,512]{2,1,0:T(8,128)(2,1)}) %tuple.50, (s32[8]{0:T(128)S(1)}, ...), branch_computations={%region_0.0_spmd, %region_1.0_spmd} | conditional | flops 1074069504 | bytes 23855476 | solution.py:528
  9.3 3.7 %branch_1_fun.7 = (f32[1,256,512]{2,1,0:T(8,128)S(1)}, bf16[1,256,512]{2,1,0:T(8,128)(2,1)S(1)}) custom-call(s32[8]{0:T(128)S(1)} %get-tuple-element.42.plan, bf16[2,2048,512]{2,1,0:T(8,128)(2,1)} %get-tuple-element.43.factors), custom_call_target="tpu_custom_call" | custom-call | flops 1073741824 | bytes 1048576 | tf_op jit(solution)/shard_map/cond/branch_1_fun/pallas_call | solution.py:513
  13.1 1.5 %collective-permute-done.came = bf16[1,256,512]{2,1,0:T(8,128)(2,1)S(1)} collective-permute-done((bf16[1,256,512]{2,1,0:T(8,128)(2,1)S(1)}, bf16[1,256,512]{2,1,0:T(8,128)(2,1)S(1)}, u32[]{:S(2)}, u32[]{:S(2)}) %collective-permute-start) | collective-permute-done | bytes 262176 | tf_op jit(solution)/shard_map/cond/branch_1_fun/ppermute | solution.py:112
  15.2 1.6 %collective-permute-start.1 = (bf16[1,128,512]{2,1,0:T(8,128)(2,1)S(1)}, bf16[1,128,512]{2,1,0:T(8,128)(2,1)S(1)}, u32[]{:S(2)}, u32[]{:S(2)}) collective-permute-start(bf16[1,128,512]{2,1,0:T(8,128)(2,1)S(1)} %get-tuple-element.47), channel_id=1, source_target_pairs={{0,2},{1,3},{2,0},{3,1},{4,6},{5,7},{6,4},{7,5},{8,10},{9,11},{10,... | collective-permute-start | bytes 393224 | tf_op jit(solution)/shard_map/cond/branch_1_fun/ppermute | solution.py:118
  16.8 4.0 %collective-permute-done.1.came = bf16[1,128,512]{2,1,0:T(8,128)(2,1)S(1)} collective-permute-done((bf16[1,128,512]{2,1,0:T(8,128)(2,1)S(1)}, bf16[1,128,512]{2,1,0:T(8,128)(2,1)S(1)}, u32[]{:S(2)}, u32[]{:S(2)}) %collective-permute-start.1) | collective-permute-done | bytes 131104 | tf_op jit(solution)/shard_map/cond/branch_1_fun/ppermute | solution.py:118
  21.4 2.7 %collective-permute-start.2 = (bf16[1,32,512]{2,1,0:T(8,128)(2,1)S(1)}, bf16[1,32,512]{2,1,0:T(8,128)(2,1)S(1)}, u32[]{:S(2)}, u32[]{:S(2)}) collective-permute-start(bf16[1,32,512]{2,1,0:T(8,128)(2,1)S(1)} %get-tuple-element.49), channel_id=1, source_target_pairs={{0,8},{1,9},{2,10},{3,11},{4,12},{5,13},{6,14},{7,15},{8,0},{9,1},... | collective-permute-start | bytes 98312 | tf_op jit(solution)/shard_map/cond/branch_1_fun/ppermute | solution.py:118
  24.0 1.6 %collective-permute-start.3 = (bf16[1,32,512]{2,1,0:T(8,128)(2,1)S(1)}, bf16[1,32,512]{2,1,0:T(8,128)(2,1)S(1)}, u32[]{:S(2)}, u32[]{:S(2)}) collective-permute-start(bf16[1,32,512]{2,1,0:T(8,128)(2,1)S(1)} %get-tuple-element.50), channel_id=1, source_target_pairs={{0,4},{1,5},{2,6},{3,7},{4,0},{5,1},{6,2},{7,3},{8,12},{9,13},{10,... | collective-permute-start | bytes 98312 | tf_op jit(solution)/shard_map/cond/branch_1_fun/ppermute | solution.py:118
  25.8 1.7 %branch_1_fun.10 = (f32[1,32,512]{2,1,0:T(8,128)S(1)}, f32[2,32,512]{2,1,0:T(8,128)S(1)}, bf16[1024,512]{1,0:T(8,128)(2,1)}) custom-call(s32[8]{0:T(128)S(1)} %get-tuple-element.42.plan, f32[4]{0:T(128)S(1)} %get-tuple-element.52.occ, f32[4,512]{1,0:T(4,128)S(1)} %get-tuple-element.53.virt, bf16[2,2048,512]{2,1,0:T(8,128)(2,1)S(1)} %copy-done.1), custom_call_target="tpu_custom_call" | custom-call | bytes 1048576 | tf_op jit(solution)/shard_map/cond/branch_1_fun/pallas_call | solution.py:500
  27.9 3.4 %collective-permute-done.4 = bf16[1,32,512]{2,1,0:T(8,128)(2,1)S(1)} collective-permute-done((bf16[1,32,512]{2,1,0:T(8,128)(2,1)S(1)}, bf16[1,32,512]{2,1,0:T(8,128)(2,1)S(1)}, u32[]{:S(2)}, u32[]{:S(2)}) %collective-permute-start.4) | collective-permute-done | bytes 32800 | tf_op jit(solution)/shard_map/cond/branch_1_fun/ppermute | solution.py:118
  31.8 4.0 %collective-permute-start.5 = (bf16[1,32,512]{2,1,0:T(8,128)(2,1)S(1)}, bf16[1,32,512]{2,1,0:T(8,128)(2,1)S(1)}, u32[]{:S(2)}, u32[]{:S(2)}) collective-permute-start(bf16[1,32,512]{2,1,0:T(8,128)(2,1)S(1)} %multiply_convert_fusion), channel_id=1, source_target_pairs={{0,8},{1,9},{2,10},{3,11},{4,12},{5,13},{6,14},{7,15},{8,0},{9,1},... | collective-permute-start | bytes 98312 | tf_op jit(solution)/shard_map/cond/branch_1_fun/ppermute | solution.py:118
  37.7 3.7 %collective-permute-done.22.got1 = bf16[1536,512]{1,0:T(8,128)(2,1)} collective-permute-done((bf16[1536,512]{1,0:T(8,128)(2,1)}, bf16[1536,512]{1,0:T(8,128)(2,1)}, u32[]{:S(2)}, u32[]{:S(2)}) %collective-permute-start.22) | collective-permute-done | bytes 1572896 | tf_op jit(solution)/shard_map/ppermute | solution.py:112
  41.4 1.7 %collective-permute-start.23 = (bf16[1024,512]{1,0:T(8,128)(2,1)}, bf16[1024,512]{1,0:T(8,128)(2,1)S(1)}, u32[]{:S(2)}, u32[]{:S(2)}) collective-permute-start(bf16[1024,512]{1,0:T(8,128)(2,1)} %get-tuple-element.106), channel_id=1, source_target_pairs={{0,16},{16,0},{1,17},{17,1},{2,18},{18,2},{3,19},{19,3},{4,20},{20... | collective-permute-start | bytes 3145736 | tf_op jit(solution)/shard_map/ppermute | solution.py:112
  43.2 27.0 %conditional.4 = (f32[2,32,512]{2,1,0:T(8,128)S(1)}, bf16[1024,512]{1,0:T(8,128)(2,1)S(1)}, bf16[8,1,32,512]{3,2,1,0:T(8,128)(2,1)}, bf16[8,1,32,512]{3,2,1,0:T(8,128)(2,1)}) conditional(s32[]{:T(128)} %convert_element_type.42, (s32[8]{0:T(128)S(1)}, bf16[2,2048,512]{2,1,0:T(8,128)(2,1)}, bf16[4,1,32,512]{3,2,1,0:T(8,128)(2,1)S(1)}) %tuple.36, ...), branch_computations={%region_2.0_spmd, %region_3.0_spmd} | conditional | flops 1342373888 | bytes 9634104 | solution.py:565
  43.2 4.2 %branch_1_fun.11 = (f32[2,256,512]{2,1,0:T(8,128)S(1)}, bf16[2,256,512]{2,1,0:T(8,128)(2,1)S(1)}, bf16[1024,512]{1,0:T(8,128)(2,1)S(1)}) custom-call(s32[8]{0:T(128)S(1)} %get-tuple-element.60.plan, bf16[2,2048,512]{2,1,0:T(8,128)(2,1)} %get-tuple-element.61.factors, bf16[1536,512]{1,0:T(8,128)(2,1)} %get-tuple-element.62.got_hbm), custom_call_target="tpu_custom_call" | custom-call | flops 1342177280 | bytes 1048576 | tf_op jit(solution)/shard_map/cond/branch_1_fun/pallas_call | solution.py:536
  47.5 1.9 %collective-permute-done.10.came = bf16[2,256,512]{2,1,0:T(8,128)(2,1)S(1)} collective-permute-done((bf16[2,256,512]{2,1,0:T(8,128)(2,1)S(1)}, bf16[2,256,512]{2,1,0:T(8,128)(2,1)S(1)}, u32[]{:S(2)}, u32[]{:S(2)}) %collective-permute-start.10) | collective-permute-done | bytes 524320 | tf_op jit(solution)/shard_map/cond/branch_1_fun/ppermute | solution.py:112
  50.0 1.6 %collective-permute-start.11 = (bf16[2,128,512]{2,1,0:T(8,128)(2,1)S(1)}, bf16[2,128,512]{2,1,0:T(8,128)(2,1)S(1)}, u32[]{:S(2)}, u32[]{:S(2)}) collective-permute-start(bf16[2,128,512]{2,1,0:T(8,128)(2,1)S(1)} %get-tuple-element.66), channel_id=1, source_target_pairs={{0,2},{1,3},{2,0},{3,1},{4,6},{5,7},{6,4},{7,5},{8,10},{9,11},{10,... | collective-permute-start | bytes 786440 | tf_op jit(solution)/shard_map/cond/branch_1_fun/ppermute | solution.py:118
  52.8 6.4 %collective-permute-done.11.came = bf16[2,128,512]{2,1,0:T(8,128)(2,1)S(1)} collective-permute-done((bf16[2,128,512]{2,1,0:T(8,128)(2,1)S(1)}, bf16[2,128,512]{2,1,0:T(8,128)(2,1)S(1)}, u32[]{:S(2)}, u32[]{:S(2)}) %collective-permute-start.11) | collective-permute-done | bytes 262176 | tf_op jit(solution)/shard_map/cond/branch_1_fun/ppermute | solution.py:118
  59.8 2.7 %collective-permute-start.12 = (bf16[2,32,512]{2,1,0:T(8,128)(2,1)S(1)}, bf16[2,32,512]{2,1,0:T(8,128)(2,1)S(1)}, u32[]{:S(2)}, u32[]{:S(2)}) collective-permute-start(bf16[2,32,512]{2,1,0:T(8,128)(2,1)S(1)} %get-tuple-element.68), channel_id=1, source_target_pairs={{0,8},{1,9},{2,10},{3,11},{4,12},{5,13},{6,14},{7,15},{8,0},{9,1},... | collective-permute-start | bytes 196616 | tf_op jit(solution)/shard_map/cond/branch_1_fun/ppermute | solution.py:118
  62.5 1.6 %collective-permute-start.13 = (bf16[2,32,512]{2,1,0:T(8,128)(2,1)S(1)}, bf16[2,32,512]{2,1,0:T(8,128)(2,1)S(1)}, u32[]{:S(2)}, u32[]{:S(2)}) collective-permute-start(bf16[2,32,512]{2,1,0:T(8,128)(2,1)S(1)} %get-tuple-element.69), channel_id=1, source_target_pairs={{0,4},{1,5},{2,6},{3,7},{4,0},{5,1},{6,2},{7,3},{8,12},{9,13},{10,... | collective-permute-start | bytes 196616 | tf_op jit(solution)/shard_map/cond/branch_1_fun/ppermute | solution.py:118
  64.9 1.4 %collective-permute-done.12 = bf16[2,32,512]{2,1,0:T(8,128)(2,1)S(1)} collective-permute-done((bf16[2,32,512]{2,1,0:T(8,128)(2,1)S(1)}, bf16[2,32,512]{2,1,0:T(8,128)(2,1)S(1)}, u32[]{:S(2)}, u32[]{:S(2)}) %collective-permute-start.12) | collective-permute-done | bytes 65568 | tf_op jit(solution)/shard_map/cond/branch_1_fun/ppermute | solution.py:118
  67.5 2.6 %collective-permute-done.14 = bf16[2,32,512]{2,1,0:T(8,128)(2,1)S(1)} collective-permute-done((bf16[2,32,512]{2,1,0:T(8,128)(2,1)S(1)}, bf16[2,32,512]{2,1,0:T(8,128)(2,1)S(1)}, u32[]{:S(2)}, u32[]{:S(2)}) %collective-permute-start.14) | collective-permute-done | bytes 65568 | tf_op jit(solution)/shard_map/cond/branch_1_fun/ppermute | solution.py:118
  70.3 4.9 %collective-permute-done.24 = bf16[2,32,512]{2,1,0:T(8,128)(2,1)S(1)} collective-permute-done((bf16[2,32,512]{2,1,0:T(8,128)(2,1)S(1)}, bf16[2,32,512]{2,1,0:T(8,128)(2,1)S(1)}, u32[]{:S(2)}, u32[]{:S(2)}) %collective-permute-start.24) | collective-permute-done | bytes 65568 | tf_op jit(solution)/shard_map/ppermute | solution.py:112
  75.3 16.2 %conditional.5 = (bf16[8,2,32,512]{3,2,1,0:T(8,128)(2,1)}, bf16[8,2,32,512]{3,2,1,0:T(8,128)(2,1)}) conditional(s32[]{:T(128)} %convert_element_type.42, () %tuple.35, bf16[2,32,512]{2,1,0:T(8,128)(2,1)S(1)} %multiply_convert_fusion.1), branch_computations={%region_4.0_spmd, %region_5.0_spmd} | conditional | flops 393216 | bytes 5505240 | solution.py:575
  75.5 4.2 %collective-permute-start.17 = (bf16[2,32,512]{2,1,0:T(8,128)(2,1)S(1)}, bf16[2,32,512]{2,1,0:T(8,128)(2,1)S(1)}, u32[]{:S(2)}, u32[]{:S(2)}) collective-permute-start(bf16[2,32,512]{2,1,0:T(8,128)(2,1)S(1)} %param.5), channel_id=1, source_target_pairs={{0,8},{1,9},{2,10},{3,11},{4,12},{5,13},{6,14},{7,15},{8,0},{9,1},... | collective-permute-start | bytes 196616 | tf_op jit(solution)/shard_map/cond/branch_1_fun/ppermute | solution.py:118
  82.1 1.5 %collective-permute-start.20 = (bf16[4,2,32,512]{3,2,1,0:T(8,128)(2,1)S(1)}, bf16[4,2,32,512]{3,2,1,0:T(8,128)(2,1)S(1)}, u32[]{:S(2)}, u32[]{:S(2)}) collective-permute-start(bf16[4,2,32,512]{3,2,1,0:T(8,128)(2,1)S(1)} %pad_maximum_fusion.1), channel_id=1, source_target_pairs={{0,2},{1,3},{2,0},{3,1},{4,6},{5,7},{6,4},{7,5},{8,10},{9,11},{10,... | collective-permute-start | bytes 786440 | tf_op jit(solution)/shard_map/cond/branch_1_fun/ppermute | solution.py:118
  85.6 3.0 %collective-permute-done.20 = bf16[4,2,32,512]{3,2,1,0:T(8,128)(2,1)S(1)} collective-permute-done((bf16[4,2,32,512]{3,2,1,0:T(8,128)(2,1)S(1)}, bf16[4,2,32,512]{3,2,1,0:T(8,128)(2,1)S(1)}, u32[]{:S(2)}, u32[]{:S(2)}) %collective-permute-start.20) | collective-permute-done | bytes 262176 | tf_op jit(solution)/shard_map/cond/branch_1_fun/ppermute | solution.py:118
  89.3 2.2 %collective-permute-done.21 = bf16[8,2,32,512]{3,2,1,0:T(8,128)(2,1)} collective-permute-done((bf16[8,2,32,512]{3,2,1,0:T(8,128)(2,1)}, bf16[8,2,32,512]{3,2,1,0:T(8,128)(2,1)}, u32[]{:S(2)}, u32[]{:S(2)}) %collective-permute-start.21) | collective-permute-done | bytes 524320 | tf_op jit(solution)/shard_map/cond/branch_1_fun/ppermute | solution.py:112
  91.6 2.7 %shard_map.47 = (bf16[256,512]{1,0:T(8,128)(2,1)S(1)}, bf16[512,512]{1,0:T(8,128)(2,1)S(1)}, bf16[512,512]{1,0:T(8,128)(2,1)S(1)}) custom-call(s32[8]{0:T(128)S(1)} %get-tuple-element.97.plan, bf16[8,2,32,512]{3,2,1,0:T(8,128)(2,1)} %get-tuple-element.112.near_hbm, bf16[8,2,32,512]{3,2,1,0:T(8,128)(2,1)} %get-tuple-element.113.far_hbm, ...), custom_call_target="tpu_custom_call" | custom-call | flops 268435456 | bytes 1048576 | tf_op jit(solution)/shard_map/pallas_call | solution.py:578
  94.2 2.0 %collective-permute-start.25 = (bf16[256,512]{1,0:T(8,128)(2,1)S(1)}, bf16[256,512]{1,0:T(8,128)(2,1)S(1)}, u32[]{:S(2)}, u32[]{:S(2)}) collective-permute-start(bf16[256,512]{1,0:T(8,128)(2,1)S(1)} %get-tuple-element.114), channel_id=1, source_target_pairs={{0,16},{16,0},{1,17},{17,1},{2,18},{18,2},{3,19},{19,3},{4,20},{20... | collective-permute-start | bytes 786440 | tf_op jit(solution)/shard_map/ppermute | solution.py:112
  96.4 8.0 %shard_map.48.gamma_in = bf16[2,2048,512]{2,1,0:T(8,128)(2,1)} custom-call(s32[8]{0:T(128)S(1)} %get-tuple-element.97.plan, bf16[8,1,32,512]{3,2,1,0:T(8,128)(2,1)} %get-tuple-element.115.near01, bf16[8,1,32,512]{3,2,1,0:T(8,128)(2,1)} %get-tuple-element.116.far01, bf16[512,512]{1,0:T(8,128)(2,1)S(1)} %get-tuple-element.117.amp0, ...), custom_call_target="tpu_custom_call" | custom-call | flops 3221225472 | bytes 1048576 | tf_op jit(solution)/shard_map/pallas_call | solution.py:592
  (54 shorter events, 15.7 us)
Async XLA Ops:
  0.0 9.2 %copy-start.2 = (f32[4,512]{1,0:T(4,128)S(1)}, f32[4,512]{1,0:T(4,128)}, u32[]{:S(2)}) copy-start(f32[4,512]{1,0:T(4,128)} %param.12) | copy-start | bytes 24580
  0.0 9.3 %copy-start.3 = (f32[4]{0:T(128)S(1)}, f32[4]{0:T(128)}, u32[]{:S(2)}) copy-start(f32[4]{0:T(128)} %param.11) | copy-start | bytes 52
  3.7 37.7 %collective-permute-start.22 = (bf16[1536,512]{1,0:T(8,128)(2,1)}, bf16[1536,512]{1,0:T(8,128)(2,1)}, u32[]{:S(2)}, u32[]{:S(2)}) collective-permute-start(bf16[1536,512]{1,0:T(8,128)(2,1)} %get-tuple-element.98), channel_id=1, source_target_pairs={{0,16},{16,0},{1,17},{17,1},{2,18},{18,2},{3,19},{19,3},{4,20},{20... | collective-permute-start | bytes 4718600 | tf_op jit(solution)/shard_map/ppermute | solution.py:112
  9.3 16.6 %copy-start.1 = (bf16[2,2048,512]{2,1,0:T(8,128)(2,1)S(1)}, bf16[2,2048,512]{2,1,0:T(8,128)(2,1)}, u32[]{:S(2)}) copy-start(bf16[2,2048,512]{2,1,0:T(8,128)(2,1)} %get-tuple-element.43.factors) | copy-start | bytes 12582916 | tf_op jit(solution)/shard_map/cond
  13.0 1.6 %collective-permute-start = (bf16[1,256,512]{2,1,0:T(8,128)(2,1)S(1)}, bf16[1,256,512]{2,1,0:T(8,128)(2,1)S(1)}, u32[]{:S(2)}, u32[]{:S(2)}) collective-permute-start(bf16[1,256,512]{2,1,0:T(8,128)(2,1)S(1)} %get-tuple-element.45), channel_id=1, source_target_pairs={{0,1},{1,0},{2,3},{3,2},{4,5},{5,4},{6,7},{7,6},{8,9},{9,8},{10,11... | collective-permute-start | bytes 786440 | tf_op jit(solution)/shard_map/cond/branch_1_fun/ppermute | solution.py:112
  15.2 5.6 %collective-permute-start.1 = (bf16[1,128,512]{2,1,0:T(8,128)(2,1)S(1)}, bf16[1,128,512]{2,1,0:T(8,128)(2,1)S(1)}, u32[]{:S(2)}, u32[]{:S(2)}) collective-permute-start(bf16[1,128,512]{2,1,0:T(8,128)(2,1)S(1)} %get-tuple-element.47), channel_id=1, source_target_pairs={{0,2},{1,3},{2,0},{3,1},{4,6},{5,7},{6,4},{7,5},{8,10},{9,11},{10,... | collective-permute-start | bytes 393224 | tf_op jit(solution)/shard_map/cond/branch_1_fun/ppermute | solution.py:118
  21.4 6.2 %collective-permute-start.2 = (bf16[1,32,512]{2,1,0:T(8,128)(2,1)S(1)}, bf16[1,32,512]{2,1,0:T(8,128)(2,1)S(1)}, u32[]{:S(2)}, u32[]{:S(2)}) collective-permute-start(bf16[1,32,512]{2,1,0:T(8,128)(2,1)S(1)} %get-tuple-element.49), channel_id=1, source_target_pairs={{0,8},{1,9},{2,10},{3,11},{4,12},{5,13},{6,14},{7,15},{8,0},{9,1},... | collective-permute-start | bytes 98312 | tf_op jit(solution)/shard_map/cond/branch_1_fun/ppermute | solution.py:118
  24.0 3.9 %collective-permute-start.3 = (bf16[1,32,512]{2,1,0:T(8,128)(2,1)S(1)}, bf16[1,32,512]{2,1,0:T(8,128)(2,1)S(1)}, u32[]{:S(2)}, u32[]{:S(2)}) collective-permute-start(bf16[1,32,512]{2,1,0:T(8,128)(2,1)S(1)} %get-tuple-element.50), channel_id=1, source_target_pairs={{0,4},{1,5},{2,6},{3,7},{4,0},{5,1},{6,2},{7,3},{8,12},{9,13},{10,... | collective-permute-start | bytes 98312 | tf_op jit(solution)/shard_map/cond/branch_1_fun/ppermute | solution.py:118
  25.6 5.7 %collective-permute-start.4 = (bf16[1,32,512]{2,1,0:T(8,128)(2,1)S(1)}, bf16[1,32,512]{2,1,0:T(8,128)(2,1)S(1)}, u32[]{:S(2)}, u32[]{:S(2)}) collective-permute-start(bf16[1,32,512]{2,1,0:T(8,128)(2,1)S(1)} %get-tuple-element.51), channel_id=1, source_target_pairs={{0,12},{1,13},{2,14},{3,15},{4,8},{5,9},{6,10},{7,11},{8,4},{9,5},... | collective-permute-start | bytes 98312 | tf_op jit(solution)/shard_map/cond/branch_1_fun/ppermute | solution.py:118
  31.4 5.8 %collective-permute-start.7 = (bf16[1,32,512]{2,1,0:T(8,128)(2,1)S(1)}, bf16[1,32,512]{2,1,0:T(8,128)(2,1)S(1)}, u32[]{:S(2)}, u32[]{:S(2)}) collective-permute-start(bf16[1,32,512]{2,1,0:T(8,128)(2,1)S(1)} %multiply_convert_fusion), channel_id=1, source_target_pairs={{0,12},{1,13},{2,14},{3,15},{4,8},{5,9},{6,10},{7,11},{8,4},{9,5},... | collective-permute-start | bytes 98312 | tf_op jit(solution)/shard_map/cond/branch_1_fun/ppermute | solution.py:118
  31.8 5.4 %collective-permute-start.6 = (bf16[1,32,512]{2,1,0:T(8,128)(2,1)S(1)}, bf16[1,32,512]{2,1,0:T(8,128)(2,1)S(1)}, u32[]{:S(2)}, u32[]{:S(2)}) collective-permute-start(bf16[1,32,512]{2,1,0:T(8,128)(2,1)S(1)} %multiply_convert_fusion), channel_id=1, source_target_pairs={{0,4},{1,5},{2,6},{3,7},{4,0},{5,1},{6,2},{7,3},{8,12},{9,13},{10,... | collective-permute-start | bytes 98312 | tf_op jit(solution)/shard_map/cond/branch_1_fun/ppermute | solution.py:118
  31.8 5.9 %collective-permute-start.5 = (bf16[1,32,512]{2,1,0:T(8,128)(2,1)S(1)}, bf16[1,32,512]{2,1,0:T(8,128)(2,1)S(1)}, u32[]{:S(2)}, u32[]{:S(2)}) collective-permute-start(bf16[1,32,512]{2,1,0:T(8,128)(2,1)S(1)} %multiply_convert_fusion), channel_id=1, source_target_pairs={{0,8},{1,9},{2,10},{3,11},{4,12},{5,13},{6,14},{7,15},{8,0},{9,1},... | collective-permute-start | bytes 98312 | tf_op jit(solution)/shard_map/cond/branch_1_fun/ppermute | solution.py:118
  41.4 28.7 %collective-permute-start.23 = (bf16[1024,512]{1,0:T(8,128)(2,1)}, bf16[1024,512]{1,0:T(8,128)(2,1)S(1)}, u32[]{:S(2)}, u32[]{:S(2)}) collective-permute-start(bf16[1024,512]{1,0:T(8,128)(2,1)} %get-tuple-element.106), channel_id=1, source_target_pairs={{0,16},{16,0},{1,17},{17,1},{2,18},{18,2},{3,19},{19,3},{4,20},{20... | collective-permute-start | bytes 3145736 | tf_op jit(solution)/shard_map/ppermute | solution.py:112
  47.4 2.0 %collective-permute-start.10 = (bf16[2,256,512]{2,1,0:T(8,128)(2,1)S(1)}, bf16[2,256,512]{2,1,0:T(8,128)(2,1)S(1)}, u32[]{:S(2)}, u32[]{:S(2)}) collective-permute-start(bf16[2,256,512]{2,1,0:T(8,128)(2,1)S(1)} %get-tuple-element.64), channel_id=1, source_target_pairs={{0,1},{1,0},{2,3},{3,2},{4,5},{5,4},{6,7},{7,6},{8,9},{9,8},{10,11... | collective-permute-start | bytes 1572872 | tf_op jit(solution)/shard_map/cond/branch_1_fun/ppermute | solution.py:112
  50.0 9.2 %collective-permute-start.11 = (bf16[2,128,512]{2,1,0:T(8,128)(2,1)S(1)}, bf16[2,128,512]{2,1,0:T(8,128)(2,1)S(1)}, u32[]{:S(2)}, u32[]{:S(2)}) collective-permute-start(bf16[2,128,512]{2,1,0:T(8,128)(2,1)S(1)} %get-tuple-element.66), channel_id=1, source_target_pairs={{0,2},{1,3},{2,0},{3,1},{4,6},{5,7},{6,4},{7,5},{8,10},{9,11},{10,... | collective-permute-start | bytes 786440 | tf_op jit(solution)/shard_map/cond/branch_1_fun/ppermute | solution.py:118
  51.6 12.7 %collective-permute-start.15 = (bf16[4,1,32,512]{3,2,1,0:T(8,128)(2,1)S(1)}, bf16[4,1,32,512]{3,2,1,0:T(8,128)(2,1)S(1)}, u32[]{:S(2)}, u32[]{:S(2)}) collective-permute-start(bf16[4,1,32,512]{3,2,1,0:T(8,128)(2,1)S(1)} %get-tuple-element.72), channel_id=1, source_target_pairs={{0,2},{1,3},{2,0},{3,1},{4,6},{5,7},{6,4},{7,5},{8,10},{9,11},{10,... | collective-permute-start | bytes 393224 | tf_op jit(solution)/shard_map/cond/branch_1_fun/ppermute | solution.py:118
  59.8 6.5 %collective-permute-start.12 = (bf16[2,32,512]{2,1,0:T(8,128)(2,1)S(1)}, bf16[2,32,512]{2,1,0:T(8,128)(2,1)S(1)}, u32[]{:S(2)}, u32[]{:S(2)}) collective-permute-start(bf16[2,32,512]{2,1,0:T(8,128)(2,1)S(1)} %get-tuple-element.68), channel_id=1, source_target_pairs={{0,8},{1,9},{2,10},{3,11},{4,12},{5,13},{6,14},{7,15},{8,0},{9,1},... | collective-permute-start | bytes 196616 | tf_op jit(solution)/shard_map/cond/branch_1_fun/ppermute | solution.py:118
  62.5 5.0 %collective-permute-start.13 = (bf16[2,32,512]{2,1,0:T(8,128)(2,1)S(1)}, bf16[2,32,512]{2,1,0:T(8,128)(2,1)S(1)}, u32[]{:S(2)}, u32[]{:S(2)}) collective-permute-start(bf16[2,32,512]{2,1,0:T(8,128)(2,1)S(1)} %get-tuple-element.69), channel_id=1, source_target_pairs={{0,4},{1,5},{2,6},{3,7},{4,0},{5,1},{6,2},{7,3},{8,12},{9,13},{10,... | collective-permute-start | bytes 196616 | tf_op jit(solution)/shard_map/cond/branch_1_fun/ppermute | solution.py:118
  64.0 6.1 %collective-permute-start.14 = (bf16[2,32,512]{2,1,0:T(8,128)(2,1)S(1)}, bf16[2,32,512]{2,1,0:T(8,128)(2,1)S(1)}, u32[]{:S(2)}, u32[]{:S(2)}) collective-permute-start(bf16[2,32,512]{2,1,0:T(8,128)(2,1)S(1)} %get-tuple-element.70), channel_id=1, source_target_pairs={{0,12},{1,13},{2,14},{3,15},{4,8},{5,9},{6,10},{7,11},{8,4},{9,5},... | collective-permute-start | bytes 196616 | tf_op jit(solution)/shard_map/cond/branch_1_fun/ppermute | solution.py:118
  64.9 5.2 %collective-permute-start.16 = (bf16[8,1,32,512]{3,2,1,0:T(8,128)(2,1)}, bf16[8,1,32,512]{3,2,1,0:T(8,128)(2,1)}, u32[]{:S(2)}, u32[]{:S(2)}) collective-permute-start(bf16[8,1,32,512]{3,2,1,0:T(8,128)(2,1)} %constant_dynamic-update-slice_fusion.2), channel_id=1, source_target_pairs={{0,1},{1,0},{2,3},{3,2},{4,5},{5,4},{6,7},{7,6},{8,9},{9,8},{10,11... | collective-permute-start | bytes 786440 | tf_op jit(solution)/shard_map/cond/branch_1_fun/ppermute | solution.py:112
  70.2 5.0 %collective-permute-start.24 = (bf16[2,32,512]{2,1,0:T(8,128)(2,1)S(1)}, bf16[2,32,512]{2,1,0:T(8,128)(2,1)S(1)}, u32[]{:S(2)}, u32[]{:S(2)}) collective-permute-start(bf16[2,32,512]{2,1,0:T(8,128)(2,1)S(1)} %convert_element_type.43), channel_id=1, source_target_pairs={{0,16},{16,0},{1,17},{17,1},{2,18},{18,2},{3,19},{19,3},{4,20},{20... | collective-permute-start | bytes 196616 | tf_op jit(solution)/shard_map/ppermute | solution.py:112
  75.2 21.3 %collective-permute-start.26 = (bf16[1024,512]{1,0:T(8,128)(2,1)S(1)}, bf16[1024,512]{1,0:T(8,128)(2,1)S(1)}, u32[]{:S(2)}, u32[]{:S(2)}) collective-permute-start(bf16[1024,512]{1,0:T(8,128)(2,1)S(1)} %get-tuple-element.120), channel_id=1, source_target_pairs={{0,16},{16,0},{1,17},{17,1},{2,18},{18,2},{3,19},{19,3},{4,20},{20... | collective-permute-start | bytes 3145736 | tf_op jit(solution)/shard_map/ppermute | solution.py:112
  75.3 6.1 %collective-permute-start.19 = (bf16[2,32,512]{2,1,0:T(8,128)(2,1)S(1)}, bf16[2,32,512]{2,1,0:T(8,128)(2,1)S(1)}, u32[]{:S(2)}, u32[]{:S(2)}) collective-permute-start(bf16[2,32,512]{2,1,0:T(8,128)(2,1)S(1)} %param.5), channel_id=1, source_target_pairs={{0,12},{1,13},{2,14},{3,15},{4,8},{5,9},{6,10},{7,11},{8,4},{9,5},... | collective-permute-start | bytes 196616 | tf_op jit(solution)/shard_map/cond/branch_1_fun/ppermute | solution.py:118
  75.5 5.9 %collective-permute-start.18 = (bf16[2,32,512]{2,1,0:T(8,128)(2,1)S(1)}, bf16[2,32,512]{2,1,0:T(8,128)(2,1)S(1)}, u32[]{:S(2)}, u32[]{:S(2)}) collective-permute-start(bf16[2,32,512]{2,1,0:T(8,128)(2,1)S(1)} %param.5), channel_id=1, source_target_pairs={{0,4},{1,5},{2,6},{3,7},{4,0},{5,1},{6,2},{7,3},{8,12},{9,13},{10,... | collective-permute-start | bytes 196616 | tf_op jit(solution)/shard_map/cond/branch_1_fun/ppermute | solution.py:118
  75.5 6.6 %collective-permute-start.17 = (bf16[2,32,512]{2,1,0:T(8,128)(2,1)S(1)}, bf16[2,32,512]{2,1,0:T(8,128)(2,1)S(1)}, u32[]{:S(2)}, u32[]{:S(2)}) collective-permute-start(bf16[2,32,512]{2,1,0:T(8,128)(2,1)S(1)} %param.5), channel_id=1, source_target_pairs={{0,8},{1,9},{2,10},{3,11},{4,12},{5,13},{6,14},{7,15},{8,0},{9,1},... | collective-permute-start | bytes 196616 | tf_op jit(solution)/shard_map/cond/branch_1_fun/ppermute | solution.py:118
  82.1 6.4 %collective-permute-start.20 = (bf16[4,2,32,512]{3,2,1,0:T(8,128)(2,1)S(1)}, bf16[4,2,32,512]{3,2,1,0:T(8,128)(2,1)S(1)}, u32[]{:S(2)}, u32[]{:S(2)}) collective-permute-start(bf16[4,2,32,512]{3,2,1,0:T(8,128)(2,1)S(1)} %pad_maximum_fusion.1), channel_id=1, source_target_pairs={{0,2},{1,3},{2,0},{3,1},{4,6},{5,7},{6,4},{7,5},{8,10},{9,11},{10,... | collective-permute-start | bytes 786440 | tf_op jit(solution)/shard_map/cond/branch_1_fun/ppermute | solution.py:118
  89.3 2.3 %collective-permute-start.21 = (bf16[8,2,32,512]{3,2,1,0:T(8,128)(2,1)}, bf16[8,2,32,512]{3,2,1,0:T(8,128)(2,1)}, u32[]{:S(2)}, u32[]{:S(2)}) collective-permute-start(bf16[8,2,32,512]{3,2,1,0:T(8,128)(2,1)} %constant_dynamic-update-slice_fusion.4), channel_id=1, source_target_pairs={{0,1},{1,0},{2,3},{3,2},{4,5},{5,4},{6,7},{7,6},{8,9},{9,8},{10,11... | collective-permute-start | bytes 1572872 | tf_op jit(solution)/shard_map/cond/branch_1_fun/ppermute | solution.py:112
  91.5 4.9 %copy-start = (bf16[2,2048,512]{2,1,0:T(8,128)(2,1)S(1)}, bf16[2,2048,512]{2,1,0:T(8,128)(2,1)}, u32[]{:S(2)}) copy-start(bf16[2,2048,512]{2,1,0:T(8,128)(2,1)} %factors.5) | copy-start | bytes 12582916
  94.2 10.2 %collective-permute-start.25 = (bf16[256,512]{1,0:T(8,128)(2,1)S(1)}, bf16[256,512]{1,0:T(8,128)(2,1)S(1)}, u32[]{:S(2)}, u32[]{:S(2)}) collective-permute-start(bf16[256,512]{1,0:T(8,128)(2,1)S(1)} %get-tuple-element.114), channel_id=1, source_target_pairs={{0,16},{16,0},{1,17},{17,1},{2,18},{18,2},{3,19},{19,3},{4,20},{20... | collective-permute-start | bytes 786440 | tf_op jit(solution)/shard_map/ppermute | solution.py:112
where the time goes:
time: 105 us
  waiting for transfers between devices  40.5 us (39%)
  starting transfers between devices  30.1 us (29%)
  Pallas kernels  26.9 us (26%)
  local copies, waits for them, and re-layouts  5.27 us (5%)
  between operations  1.97 us (2%)
    ppermute x16, waiting for transfers between devices, direct(): return lax.ppermute(value, 'aux', [(i, i ^ mask) for i in range(size)])  26 us
    ppermute x16, starting transfers between devices, direct(): return lax.ppermute(value, 'aux', [(i, i ^ mask) for i in range(size)])  23 us
    ppermute x9, waiting for transfers between devices, swap(): return lax.ppermute(value, axis, [(i, i ^ 1 << bit) for i in range(size)])  14.5 us
    pallas_call x1, Pallas kernels, two_groups(): call(functools.partial(last_kernel, step), array(*factors.shape), [SMEM_S...  8.01 us
    ppermute x9, starting transfers between devices, swap(): return lax.ppermute(value, axis, [(i, i ^ 1 << bit) for i in range(size)])  7.12 us
    pallas_call x1, Pallas kernels, pair_chain(): call(functools.partial(pair_kernel, step), (*halves(2), array(4 * unit, w...  4.21 us
    pallas_call x1, Pallas kernels, own_chain(): call(functools.partial(own_kernel, step), halves(1), [SMEM_SPEC, HBM_SPEC...  3.7 us
    pallas_call x1, Pallas kernels, two_groups(): call(functools.partial(plan_kernel, tile_table.shape[0], bits, step), (ar...  3.66 us
  transfers between devices with their start and end apart: 25, of which 18 were waited for; matrix products, arithmetic and copies ran while one was open for 5% of the time, Pallas kernels for 22%

commit v1 on v0

--- a/solution.py
+++ b/solution.py
@@ -208,17 +208,26 @@
     wait_all(second for _, second in copies)
 
 
-def weigh_kernel(step, plan, occ, virt, factors, own_weight, weights, pay_a, stage, sems):
+def weigh_kernel(step, plan, occ, virt, factors, own_weight, weights, pay_a, pay_b, stage, sems):
+    piece = step // 4
     helps, foreign = plan[HELPS], plan[FOREIGN]
     b0, b1 = jnp.where(helps == 1, 0, foreign), jnp.where(helps == 1, 1, foreign)
+    moves = (
+        (b1, 12 - 4 * helps, 4, pay_a, 0, 0),
+        (b0, 4, 4, pay_a, 4, 4),
+        (b1, 7, 1, pay_a, 8, 8),
+        (b1, 4, 3, pay_b, 0, 9),
+        (b0, 2, 2, pay_b, 3, 12),
+        (b1, 2, 2, pay_b, 5, 14),
+    )
     copies = [
         staged(
-            factors.at[block, rows_at(step, start, 1)],
-            stage.at[pl.ds(n * step, step)],
-            pay_a.at[pl.ds(n * step, step)],
+            factors.at[block, rows_at(piece, start, size)],
+            stage.at[pl.ds(between * piece, size * piece)],
+            pay.at[pl.ds(to * piece, size * piece)],
             sems.at[n],
         )
-        for n, (block, start) in enumerate(((b1, 3 - helps), (b0, 1)))
+        for n, (block, start, size, pay, to, between) in enumerate(moves)
     ]
     start_all(first for first, _ in copies)
     low, partner = plan[LOW], plan[PARTNER]
@@ -235,27 +244,6 @@
     wait_all(second for _, second in copies)
 
 
-def third_rows(unit, plan, factors, pay_b, stage, sems):
-    helps, foreign = plan[HELPS], plan[FOREIGN]
-    b0, b1 = jnp.where(helps == 1, 0, foreign), jnp.where(helps == 1, 1, foreign)
-    return [
-        staged(
-            factors.at[block, pl.ds(start * unit, size * unit)],
-            stage.at[pl.ds(to * unit, size * unit)],
-            pay_b.at[pl.ds(to * unit, size * unit)],
-            sems.at[n],
-        )
-        for n, (block, start, size, to) in enumerate(((b1, 2, 2, 0), (b0, 1, 1, 2), (b1, 1, 1, 3)))
-    ]
-
-
-def pack_kernel(unit, plan, factors, pay_b, stage, sems):
-    copies = third_rows(unit, plan, factors, pay_b, stage, sems)
-    start_all(first for first, _ in copies)
-    relay(copies)
-    wait_all(second for _, second in copies)
-
-
 def split_halves(acc, pair, kept, sent, core):
     half = kept.shape[1]
     kept[pair] = acc[pl.ds(pl.multiple_of(core * half, half), half), :]
@@ -280,7 +268,7 @@
 
 
 def pair_kernel(
-    step, plan, factors, got_hbm, kept, sent, pay_b, got, rows0, rows1, acc0, acc1, stage, sems, pay_sems
+    step, plan, factors, got_hbm, kept, sent, got, rows0, rows1, acc0, acc1, sems
 ):
     helps, foreign = plan[HELPS], plan[FOREIGN]
     b0, b1 = jnp.where(helps == 1, 0, foreign), jnp.where(helps == 1, 1, foreign)
@@ -301,8 +289,6 @@
         for n in range(3)
     ]
     start_all((gots[0], copies0[0], gots[1], copies0[1], gots[2], copies1[2], *copies1[:2]))
-    pays = third_rows(step // 2, plan, factors, pay_b, stage, pay_sems)
-    start_all(first for first, _ in pays)
 
     for n in range(2):
         wait_all((gots[n], copies0[n]))
@@ -328,7 +314,6 @@
         acc1[...] = outer(cut(got, 2), cut(rows1, 2))
 
     wait_all(copies1[:2])
-    relay(pays)
 
     @pl.when(helps == 1)
     def _():
@@ -337,7 +322,6 @@
     core = lax.axis_index("aux") & 1
     split_halves(acc0, 0, kept, sent, core)
     split_halves(acc1, 1, kept, sent, core)
-    wait_all(second for _, second in pays)
 
 
 def arrange(plan, near, far, pair, out):
@@ -348,17 +332,12 @@
             out[pl.ds(row, shard), :] = source[n, pair]
 
 
-def back_kernel(plan, near_hbm, far_hbm, factors, back, amp0, amp1, wide, rows, sems):
-    unit = back.shape[0]
-    copies = [
-        pltpu.make_async_copy(near_hbm, wide.at[0], sems.at[0]),
-        pltpu.make_async_copy(far_hbm, wide.at[1], sems.at[1]),
-        pltpu.make_async_copy(factors.at[:, pl.ds(0, unit)], rows, sems.at[2]),
-    ]
-    start_all(copies)
-    wait_all(copies)
-    arrange(plan, wide.at[0], wide.at[1], 0, amp0)
-    arrange(plan, wide.at[0], wide.at[1], 1, amp1)
+def back_kernel(plan, near, far, factors, back, amp0, amp1, rows, sem):
+    copy = pltpu.make_async_copy(factors.at[:, pl.ds(0, back.shape[0])], rows, sem)
+    copy.start()
+    arrange(plan, near, far, 0, amp0)
+    arrange(plan, near, far, 1, amp1)
+    copy.wait()
     total = right(rows[0], amp0[...]) + right(rows[1], amp1[...])
     back[...] = total.astype(back.dtype)
 
@@ -366,7 +345,7 @@
 def last_kernel(
     step, plan, near01, far01, amp0, amp1, got1, got_a, got_b, factors, gamma, small, rows, own, out, own_amp, ins, outs
 ):
-    unit = step // 2
+    unit, piece = step // 2, step // 4
     foreign = plan[FOREIGN]
 
     def part(start, size):
@@ -403,8 +382,10 @@
     def _():
         others = [
             copy(got1, rows.at[part(0, 6)], 4),
-            copy(got_a, rows.at[part(6, 4)], 5),
-            copy(got_b, rows.at[part(10, 4)], 6),
+            copy(got_a.at[part(0, 4)], rows.at[part(6, 4)], 5),
+            copy(got_a.at[pl.ds(8 * piece, piece)], rows.at[pl.ds(23 * piece, piece)], 6),
+            copy(got_b.at[pl.ds(0, 3 * piece)], rows.at[pl.ds(20 * piece, 3 * piece)], 7),
+            copy(got_b.at[pl.ds(3 * piece, 4 * piece)], rows.at[part(12, 2)], 8),
         ]
         start_all(others)
         out[0] = jnp.zeros_like(out[0])
@@ -502,11 +483,12 @@
             (
                 array(1, shard, width, dtype=jnp.float32),
                 array(2, shard, width, dtype=jnp.float32),
-                array(2 * step, width),
+                array(9 * step // 4, width),
+                array(7 * step // 4, width),
             ),
             [SMEM_SPEC, SMEM_SPEC, VMEM_SPEC, HBM_SPEC],
-            (VMEM_SPEC, VMEM_SPEC, HBM_SPEC),
-            [pltpu.VMEM((2 * step, width), dtype), dma((2, 2))],
+            (VMEM_SPEC, VMEM_SPEC, HBM_SPEC, HBM_SPEC),
+            [pltpu.VMEM((4 * step, width), dtype), dma((6, 2))],
         )(plan, occ_energy, virt_energy, factors)
 
     def own_chain():
@@ -518,14 +500,14 @@
             [pltpu.VMEM(factors.shape, dtype), square, dma((4,))],
             4,
         )(plan, factors)
-        own_weight, weights, pay_a = prepare()
+        own_weight, weights, pay_a, pay_b = prepare()
         shards01 = (scatter(kept, sent) * own_weight).astype(dtype)
-        return gather_lower(shards01, bits), weights, pay_a
+        return gather_lower(shards01, bits), weights, pay_a, pay_b
 
     def no_chain():
         return jnp.zeros((aux // 4, 1, shard, width), dtype), *prepare()[1:]
 
-    part01, weights, pay_a = lax.cond(plan[COUNTS] > 0, own_chain, no_chain)
+    part01, weights, pay_a, pay_b = lax.cond(plan[COUNTS] > 0, own_chain, no_chain)
     used = plan[COUNTS + 1] + plan[COUNTS + 2] > 0
     got1, part01, weights, pay_a, used = lax.optimization_barrier(
         (got1, part01, weights, pay_a, used)
@@ -533,60 +515,50 @@
     got_a = swap(pay_a, "orb", 0)
 
     def pair_chain():
-        kept, sent, pay_b = call(
+        kept, sent = call(
             functools.partial(pair_kernel, step),
-            (*halves(2), array(4 * unit, width)),
+            halves(2),
             [SMEM_SPEC, HBM_SPEC, HBM_SPEC],
-            (VMEM_SPEC, VMEM_SPEC, HBM_SPEC),
+            (VMEM_SPEC, VMEM_SPEC),
             [
                 pltpu.VMEM((3 * step, width), dtype),
                 pltpu.VMEM((2 * step, width), dtype),
                 pltpu.VMEM((3 * step, width), dtype),
                 square,
                 square,
-                pltpu.VMEM((4 * unit, width), dtype),
                 dma((8,)),
-                dma((3, 2)),
             ],
             5,
         )(plan, factors, got1)
-        return scatter(kept, sent), pay_b, *gather(part01, bits)
+        return scatter(kept, sent), *gather(part01, bits)
 
     def no_pairs():
-        pay_b = call(
-            functools.partial(pack_kernel, unit),
-            array(4 * unit, width),
-            [SMEM_SPEC, HBM_SPEC],
-            HBM_SPEC,
-            [pltpu.VMEM((4 * unit, width), dtype), dma((3, 2))],
-        )(plan, factors)
-        return jnp.zeros((2, shard, width), jnp.float32), pay_b, *gather(part01, bits)
-
-    sums, pay_b, near01, far01 = lax.cond(used, pair_chain, no_pairs)
+        return jnp.zeros((2, shard, width), jnp.float32), *gather(part01, bits)
+
+    sums, near01, far01 = lax.cond(used, pair_chain, no_pairs)
     sums, got_a, pay_b = lax.optimization_barrier((sums, got_a, pay_b))
     sums = sums + swap(sums.astype(WIRE), "orb", 0).astype(jnp.float32)
     shards0, pay_b = lax.optimization_barrier(((sums * weights).astype(dtype), pay_b))
     got_b = swap(pay_b, "orb", 0)
 
+    amp = array(width, width)
+
+    def amplitudes():
+        near, far = gather(gather_lower(shards0, bits), bits)
+        return call(
+            back_kernel,
+            (array(unit, width), amp, amp),
+            [SMEM_SPEC, VMEM_SPEC, VMEM_SPEC, HBM_SPEC],
+            (VMEM_SPEC,) * 3,
+            [pltpu.VMEM((2, unit, width), dtype), dma],
+            1,
+        )(plan, near, far, factors)
+
     def nothing():
-        half = jnp.zeros((aux // 2, 2, shard, width), dtype)
-        return half, half
-
-    near, far = lax.cond(used, lambda: gather(gather_lower(shards0, bits), bits), nothing)
-
-    amp = array(width, width)
-    back, amp0, amp1 = call(
-        back_kernel,
-        (array(unit, width), amp, amp),
-        [SMEM_SPEC] + [HBM_SPEC] * 3,
-        (VMEM_SPEC,) * 3,
-        [
-            pltpu.VMEM((2, *near.shape), dtype),
-            pltpu.VMEM((2, unit, width), dtype),
-            dma((3,)),
-        ],
-        1,
-    )(plan, near, far, factors)
+        zeros = jnp.zeros((width, width), dtype)
+        return jnp.zeros((unit, width), dtype), zeros, zeros
+
+    back, amp0, amp1 = lax.cond(used, amplitudes, nothing)
     got_back = swap(back, "orb", 0)
 
     gamma = call(
@@ -622,7 +594,7 @@
     simple = groups == 2 and factors.shape[0] == 2 and tile_table.shape[0] <= CAP
     width = factors.shape[2]
     whole_shards = aux >= 4 and aux & (aux - 1) == 0 and width % (32 * aux) == 0
-    if simple and whole_shards and factors.shape[1] % 128 == 0:
+    if simple and whole_shards and factors.shape[1] % 256 == 0:
         return two_groups(factors, occ_energy, virt_energy, tile_table)
     return general(factors, occ_energy, virt_energy, tile_table)
 

time: 105 us -> 104 us (level)
  waiting for transfers between devices: 40.5 us -> 44.5 us
  local copies, waits for them, and re-layouts: 5.27 us -> 2.04 us
  Pallas kernels: 26.9 us -> 23.7 us
  starting transfers between devices: 30.1 us -> 31.2 us
    pallas_call x1, Pallas kernels: 8.01 us -> 4.89 us  [two_groups(): call(functools.partial(last_kernel, step), array(*factors.shape), [SMEM_S...]
    ppermute x16, waiting for transfers between devices: 26 us -> 28.9 us  [direct(): return lax.ppermute(value, 'aux', [(i, i ^ mask) for i in range(size)])]
    cond x7, local copies, waits for them, and re-layouts: 3.22 us -> 0.69 us
    pallas_call x2, Pallas kernels: 6.88 us -> 5.44 us  [the longest x1 3.34 us: pair_chain(): call(functools.partial(pair_kernel, step), halves(2), [SMEM_SPEC, HBM_SPE...]
    ppermute x9, starting transfers between devices: 7.12 us -> 8.26 us  [swap(): return lax.ppermute(value, axis, [(i, i ^ 1 << bit) for i in range(size)])]
    ppermute x9, waiting for transfers between devices: 14.5 us -> 15.6 us  [swap(): return lax.ppermute(value, axis, [(i, i ^ 1 << bit) for i in range(size)])]
  transfers between devices with their start and end apart: 25 -> 25, of which waited for: 18 -> 18; matrix products, arithmetic and copies ran while one was open for 5% -> 2% of each run, Pallas kernels for 22% -> 18%
where the time goes in v1:
time: 104 us
  waiting for transfers between devices  44.5 us (43%)
  starting transfers between devices  31.2 us (30%)
  Pallas kernels  23.7 us (23%)
  local copies, waits for them, and re-layouts  2.04 us (2%)
  between operations  1.95 us (2%)
    ppermute x16, waiting for transfers between devices, direct(): return lax.ppermute(value, 'aux', [(i, i ^ mask) for i in range(size)])  28.9 us
    ppermute x16, starting transfers between devices, direct(): return lax.ppermute(value, 'aux', [(i, i ^ mask) for i in range(size)])  23 us
    ppermute x9, waiting for transfers between devices, swap(): return lax.ppermute(value, axis, [(i, i ^ 1 << bit) for i in range(size)])  15.6 us
    ppermute x9, starting transfers between devices, swap(): return lax.ppermute(value, axis, [(i, i ^ 1 << bit) for i in range(size)])  8.26 us
    pallas_call x1, Pallas kernels, two_groups(): call(functools.partial(last_kernel, step), array(*factors.shape), [SMEM_S...  4.89 us
    pallas_call x1, Pallas kernels, own_chain(): call(functools.partial(own_kernel, step), halves(1), [SMEM_SPEC, HBM_SPEC...  3.69 us
    pallas_call x1, Pallas kernels, two_groups(): call(functools.partial(plan_kernel, tile_table.shape[0], bits, step), (ar...  3.66 us
    pallas_call x1, Pallas kernels, pair_chain(): call(functools.partial(pair_kernel, step), halves(2), [SMEM_SPEC, HBM_SPE...  3.34 us
  transfers between devices with their start and end apart: 25, of which 18 were waited for; matrix products, arithmetic and copies ran while one was open for 2% of the time, Pallas kernels for 18%

profile of v1, /device:TPU:0, one launch (start us, length us, event | category | flops | bytes accessed | tf_op | source)
XLA Modules:
  0.0 103.7 jit_solution(16052597013891077265)
XLA Ops:
  0.0 3.7 %shard_map.46 = (s32[8]{0:T(128)S(1)}, bf16[1536,512]{1,0:T(8,128)(2,1)}) custom-call(s32[4,3]{1,0:T(4,128)} %table.1, bf16[2,2048,512]{2,1,0:T(8,128)(2,1)} %factors.3), custom_call_target="tpu_custom_call" | custom-call | bytes 1048576 | tf_op jit(solution)/shard_map/pallas_call | solution.py:445
  3.7 3.0 %collective-permute-start.22 = (bf16[1536,512]{1,0:T(8,128)(2,1)}, bf16[1536,512]{1,0:T(8,128)(2,1)}, u32[]{:S(2)}, u32[]{:S(2)}) collective-permute-start(bf16[1536,512]{1,0:T(8,128)(2,1)} %get-tuple-element.97), channel_id=1, source_target_pairs={{0,16},{16,0},{1,17},{17,1},{2,18},{18,2},{3,19},{19,3},{4,20},{20... | collective-permute-start | bytes 4718600 | tf_op jit(solution)/shard_map/ppermute | solution.py:112
  9.3 28.4 %conditional.3 = (bf16[4,1,32,512]{3,2,1,0:T(8,128)(2,1)S(1)}, f32[2,32,512]{2,1,0:T(8,128)S(1)}, bf16[1152,512]{1,0:T(8,128)(2,1)S(1)}, bf16[896,512]{1,0:T(8,128)(2,1)}) conditional(s32[]{:T(128)} %bitcast.8, (s32[8]{0:T(128)S(1)}, f32[4]{0:T(128)S(1)}, f32[4,512]{1,0:T(4,128)S(1)}, bf16[2,2048,512]{2,1,0:T(8,128)(2,1)}) %tuple.51, ...), branch_computations={%region_0.0_spmd, %region_1.0_spmd} | conditional | flops 1074069504 | bytes 23855484 | solution.py:510
  9.3 3.7 %branch_1_fun.8 = (f32[1,256,512]{2,1,0:T(8,128)S(1)}, bf16[1,256,512]{2,1,0:T(8,128)(2,1)S(1)}) custom-call(s32[8]{0:T(128)S(1)} %get-tuple-element.43.plan, bf16[2,2048,512]{2,1,0:T(8,128)(2,1)} %get-tuple-element.44.factors), custom_call_target="tpu_custom_call" | custom-call | flops 1073741824 | bytes 1048576 | tf_op jit(solution)/shard_map/cond/branch_1_fun/pallas_call | solution.py:495
  15.2 1.6 %collective-permute-start.1 = (bf16[1,128,512]{2,1,0:T(8,128)(2,1)S(1)}, bf16[1,128,512]{2,1,0:T(8,128)(2,1)S(1)}, u32[]{:S(2)}, u32[]{:S(2)}) collective-permute-start(bf16[1,128,512]{2,1,0:T(8,128)(2,1)S(1)} %get-tuple-element.48), channel_id=1, source_target_pairs={{0,2},{1,3},{2,0},{3,1},{4,6},{5,7},{6,4},{7,5},{8,10},{9,11},{10,... | collective-permute-start | bytes 393224 | tf_op jit(solution)/shard_map/cond/branch_1_fun/ppermute | solution.py:118
  16.8 4.0 %collective-permute-done.1.came = bf16[1,128,512]{2,1,0:T(8,128)(2,1)S(1)} collective-permute-done((bf16[1,128,512]{2,1,0:T(8,128)(2,1)S(1)}, bf16[1,128,512]{2,1,0:T(8,128)(2,1)S(1)}, u32[]{:S(2)}, u32[]{:S(2)}) %collective-permute-start.1) | collective-permute-done | bytes 131104 | tf_op jit(solution)/shard_map/cond/branch_1_fun/ppermute | solution.py:118
  21.4 2.7 %collective-permute-start.2 = (bf16[1,32,512]{2,1,0:T(8,128)(2,1)S(1)}, bf16[1,32,512]{2,1,0:T(8,128)(2,1)S(1)}, u32[]{:S(2)}, u32[]{:S(2)}) collective-permute-start(bf16[1,32,512]{2,1,0:T(8,128)(2,1)S(1)} %get-tuple-element.50), channel_id=1, source_target_pairs={{0,8},{1,9},{2,10},{3,11},{4,12},{5,13},{6,14},{7,15},{8,0},{9,1},... | collective-permute-start | bytes 98312 | tf_op jit(solution)/shard_map/cond/branch_1_fun/ppermute | solution.py:118
  24.0 1.6 %collective-permute-start.3 = (bf16[1,32,512]{2,1,0:T(8,128)(2,1)S(1)}, bf16[1,32,512]{2,1,0:T(8,128)(2,1)S(1)}, u32[]{:S(2)}, u32[]{:S(2)}) collective-permute-start(bf16[1,32,512]{2,1,0:T(8,128)(2,1)S(1)} %get-tuple-element.51), channel_id=1, source_target_pairs={{0,4},{1,5},{2,6},{3,7},{4,0},{5,1},{6,2},{7,3},{8,12},{9,13},{10,... | collective-permute-start | bytes 98312 | tf_op jit(solution)/shard_map/cond/branch_1_fun/ppermute | solution.py:118
  25.8 2.4 %branch_1_fun.11 = (f32[1,32,512]{2,1,0:T(8,128)S(1)}, f32[2,32,512]{2,1,0:T(8,128)S(1)}, bf16[1152,512]{1,0:T(8,128)(2,1)S(1)}, bf16[896,512]{1,0:T(8,128)(2,1)}) custom-call(s32[8]{0:T(128)S(1)} %get-tuple-element.43.plan, f32[4]{0:T(128)S(1)} %get-tuple-element.53.occ, f32[4,512]{1,0:T(4,128)S(1)} %get-tuple-element.54.virt, bf16[2,2048,512]{2,1,0:T(8,128)(2,1)S(1)} %copy-done), custom_call_target="tpu_custom_call" | custom-call | bytes 1048576 | tf_op jit(solution)/shard_map/cond/branch_1_fun/pallas_call | solution.py:481
  28.3 3.0 %collective-permute-done.4 = bf16[1,32,512]{2,1,0:T(8,128)(2,1)S(1)} collective-permute-done((bf16[1,32,512]{2,1,0:T(8,128)(2,1)S(1)}, bf16[1,32,512]{2,1,0:T(8,128)(2,1)S(1)}, u32[]{:S(2)}, u32[]{:S(2)}) %collective-permute-start.4) | collective-permute-done | bytes 32800 | tf_op jit(solution)/shard_map/cond/branch_1_fun/ppermute | solution.py:118
  32.0 3.8 %collective-permute-start.5 = (bf16[1,32,512]{2,1,0:T(8,128)(2,1)S(1)}, bf16[1,32,512]{2,1,0:T(8,128)(2,1)S(1)}, u32[]{:S(2)}, u32[]{:S(2)}) collective-permute-start(bf16[1,32,512]{2,1,0:T(8,128)(2,1)S(1)} %multiply_convert_fusion), channel_id=1, source_target_pairs={{0,8},{1,9},{2,10},{3,11},{4,12},{5,13},{6,14},{7,15},{8,0},{9,1},... | collective-permute-start | bytes 98312 | tf_op jit(solution)/shard_map/cond/branch_1_fun/ppermute | solution.py:118
  37.7 3.7 %collective-permute-done.22.got1 = bf16[1536,512]{1,0:T(8,128)(2,1)} collective-permute-done((bf16[1536,512]{1,0:T(8,128)(2,1)}, bf16[1536,512]{1,0:T(8,128)(2,1)}, u32[]{:S(2)}, u32[]{:S(2)}) %collective-permute-start.22) | collective-permute-done | bytes 1572896 | tf_op jit(solution)/shard_map/ppermute | solution.py:112
  41.4 1.7 %collective-permute-start.23 = (bf16[1152,512]{1,0:T(8,128)(2,1)S(1)}, bf16[1152,512]{1,0:T(8,128)(2,1)S(1)}, u32[]{:S(2)}, u32[]{:S(2)}) collective-permute-start(bf16[1152,512]{1,0:T(8,128)(2,1)S(1)} %get-tuple-element.105), channel_id=1, source_target_pairs={{0,16},{16,0},{1,17},{17,1},{2,18},{18,2},{3,19},{19,3},{4,20},{20... | collective-permute-start | bytes 3538952 | tf_op jit(solution)/shard_map/ppermute | solution.py:112
  43.2 26.1 %conditional.4 = (f32[2,32,512]{2,1,0:T(8,128)S(1)}, bf16[8,1,32,512]{3,2,1,0:T(8,128)(2,1)}, bf16[8,1,32,512]{3,2,1,0:T(8,128)(2,1)}) conditional(s32[]{:T(128)} %convert_element_type.42, bf16[4,1,32,512]{3,2,1,0:T(8,128)(2,1)S(1)} %get-tuple-element.102, (s32[8]{0:T(128)S(1)}, bf16[2,2048,512]{2,1,0:T(8,128)(2,1)}, bf16[1536,512]{1,0:T(8,128)(2,1)}, ...), branch_computations={%region_2.0_spmd, %region_3.0_spmd} | conditional | flops 1342373888 | bytes 9634096 | solution.py:538
  43.2 3.3 %branch_1_fun.12 = (f32[2,256,512]{2,1,0:T(8,128)S(1)}, bf16[2,256,512]{2,1,0:T(8,128)(2,1)S(1)}) custom-call(s32[8]{0:T(128)S(1)} %get-tuple-element.59.plan, bf16[2,2048,512]{2,1,0:T(8,128)(2,1)} %get-tuple-element.60.factors, bf16[1536,512]{1,0:T(8,128)(2,1)} %get-tuple-element.61.got_hbm), custom_call_target="tpu_custom_call" | custom-call | flops 1342177280 | bytes 1048576 | tf_op jit(solution)/shard_map/cond/branch_1_fun/pallas_call | solution.py:518
  46.6 1.9 %collective-permute-done.10.came = bf16[2,256,512]{2,1,0:T(8,128)(2,1)S(1)} collective-permute-done((bf16[2,256,512]{2,1,0:T(8,128)(2,1)S(1)}, bf16[2,256,512]{2,1,0:T(8,128)(2,1)S(1)}, u32[]{:S(2)}, u32[]{:S(2)}) %collective-permute-start.10) | collective-permute-done | bytes 524320 | tf_op jit(solution)/shard_map/cond/branch_1_fun/ppermute | solution.py:112
  49.1 1.6 %collective-permute-start.11 = (bf16[2,128,512]{2,1,0:T(8,128)(2,1)S(1)}, bf16[2,128,512]{2,1,0:T(8,128)(2,1)S(1)}, u32[]{:S(2)}, u32[]{:S(2)}) collective-permute-start(bf16[2,128,512]{2,1,0:T(8,128)(2,1)S(1)} %get-tuple-element.65), channel_id=1, source_target_pairs={{0,2},{1,3},{2,0},{3,1},{4,6},{5,7},{6,4},{7,5},{8,10},{9,11},{10,... | collective-permute-start | bytes 786440 | tf_op jit(solution)/shard_map/cond/branch_1_fun/ppermute | solution.py:118
  51.9 6.5 %collective-permute-done.11.came = bf16[2,128,512]{2,1,0:T(8,128)(2,1)S(1)} collective-permute-done((bf16[2,128,512]{2,1,0:T(8,128)(2,1)S(1)}, bf16[2,128,512]{2,1,0:T(8,128)(2,1)S(1)}, u32[]{:S(2)}, u32[]{:S(2)}) %collective-permute-start.11) | collective-permute-done | bytes 262176 | tf_op jit(solution)/shard_map/cond/branch_1_fun/ppermute | solution.py:118
  58.9 2.7 %collective-permute-start.12 = (bf16[2,32,512]{2,1,0:T(8,128)(2,1)S(1)}, bf16[2,32,512]{2,1,0:T(8,128)(2,1)S(1)}, u32[]{:S(2)}, u32[]{:S(2)}) collective-permute-start(bf16[2,32,512]{2,1,0:T(8,128)(2,1)S(1)} %get-tuple-element.67), channel_id=1, source_target_pairs={{0,8},{1,9},{2,10},{3,11},{4,12},{5,13},{6,14},{7,15},{8,0},{9,1},... | collective-permute-start | bytes 196616 | tf_op jit(solution)/shard_map/cond/branch_1_fun/ppermute | solution.py:118
  61.6 1.6 %collective-permute-start.13 = (bf16[2,32,512]{2,1,0:T(8,128)(2,1)S(1)}, bf16[2,32,512]{2,1,0:T(8,128)(2,1)S(1)}, u32[]{:S(2)}, u32[]{:S(2)}) collective-permute-start(bf16[2,32,512]{2,1,0:T(8,128)(2,1)S(1)} %get-tuple-element.68), channel_id=1, source_target_pairs={{0,4},{1,5},{2,6},{3,7},{4,0},{5,1},{6,2},{7,3},{8,12},{9,13},{10,... | collective-permute-start | bytes 196616 | tf_op jit(solution)/shard_map/cond/branch_1_fun/ppermute | solution.py:118
  66.6 2.6 %collective-permute-done.14 = bf16[2,32,512]{2,1,0:T(8,128)(2,1)S(1)} collective-permute-done((bf16[2,32,512]{2,1,0:T(8,128)(2,1)S(1)}, bf16[2,32,512]{2,1,0:T(8,128)(2,1)S(1)}, u32[]{:S(2)}, u32[]{:S(2)}) %collective-permute-start.14) | collective-permute-done | bytes 65568 | tf_op jit(solution)/shard_map/cond/branch_1_fun/ppermute | solution.py:118
  70.6 3.6 %collective-permute-done.24 = bf16[2,32,512]{2,1,0:T(8,128)(2,1)S(1)} collective-permute-done((bf16[2,32,512]{2,1,0:T(8,128)(2,1)S(1)}, bf16[2,32,512]{2,1,0:T(8,128)(2,1)S(1)}, u32[]{:S(2)}, u32[]{:S(2)}) %collective-permute-start.24) | collective-permute-done | bytes 65568 | tf_op jit(solution)/shard_map/ppermute | solution.py:112
  75.7 18.4 %conditional.5 = ((bf16[256,512]{1,0:T(8,128)(2,1)S(1)}, bf16[512,512]{1,0:T(8,128)(2,1)S(1)}, bf16[512,512]{1,0:T(8,128)(2,1)S(1)})) conditional(s32[]{:T(128)} %convert_element_type.42, () %tuple.34, (bf16[2,32,512]{2,1,0:T(8,128)(2,1)S(1)}, s32[8]{0:T(128)S(1)}, bf16[2,2048,512]{2,1,0:T(8,128)(2,1)}) %tuple.38), branch_computations={%region_4.0_spmd, %region_5.0_spmd} | conditional | flops 268828672 | bytes 6553808 | solution.py:561
  75.7 2.6 %collective-permute-start.19 = (bf16[2,32,512]{2,1,0:T(8,128)(2,1)S(1)}, bf16[2,32,512]{2,1,0:T(8,128)(2,1)S(1)}, u32[]{:S(2)}, u32[]{:S(2)}) collective-permute-start(bf16[2,32,512]{2,1,0:T(8,128)(2,1)S(1)} %get-tuple-element.72), channel_id=1, source_target_pairs={{0,12},{1,13},{2,14},{3,15},{4,8},{5,9},{6,10},{7,11},{8,4},{9,5},... | collective-permute-start | bytes 196616 | tf_op jit(solution)/shard_map/cond/branch_1_fun/ppermute | solution.py:118
  78.3 1.8 %collective-permute-start.17 = (bf16[2,32,512]{2,1,0:T(8,128)(2,1)S(1)}, bf16[2,32,512]{2,1,0:T(8,128)(2,1)S(1)}, u32[]{:S(2)}, u32[]{:S(2)}) collective-permute-start(bf16[2,32,512]{2,1,0:T(8,128)(2,1)S(1)} %get-tuple-element.72), channel_id=1, source_target_pairs={{0,8},{1,9},{2,10},{3,11},{4,12},{5,13},{6,14},{7,15},{8,0},{9,1},... | collective-permute-start | bytes 196616 | tf_op jit(solution)/shard_map/cond/branch_1_fun/ppermute | solution.py:118
  80.1 1.7 %collective-permute-done.19 = bf16[2,32,512]{2,1,0:T(8,128)(2,1)S(1)} collective-permute-done((bf16[2,32,512]{2,1,0:T(8,128)(2,1)S(1)}, bf16[2,32,512]{2,1,0:T(8,128)(2,1)S(1)}, u32[]{:S(2)}, u32[]{:S(2)}) %collective-permute-start.19) | collective-permute-done | bytes 65568 | tf_op jit(solution)/shard_map/cond/branch_1_fun/ppermute | solution.py:118
  83.5 1.6 %collective-permute-start.20 = (bf16[4,2,32,512]{3,2,1,0:T(8,128)(2,1)S(1)}, bf16[4,2,32,512]{3,2,1,0:T(8,128)(2,1)S(1)}, u32[]{:S(2)}, u32[]{:S(2)}) collective-permute-start(bf16[4,2,32,512]{3,2,1,0:T(8,128)(2,1)S(1)} %pad_maximum_fusion.1), channel_id=1, source_target_pairs={{0,2},{1,3},{2,0},{3,1},{4,6},{5,7},{6,4},{7,5},{8,10},{9,11},{10,... | collective-permute-start | bytes 786440 | tf_op jit(solution)/shard_map/cond/branch_1_fun/ppermute | solution.py:118
  85.1 4.9 %collective-permute-done.20 = bf16[4,2,32,512]{3,2,1,0:T(8,128)(2,1)S(1)} collective-permute-done((bf16[4,2,32,512]{3,2,1,0:T(8,128)(2,1)S(1)}, bf16[4,2,32,512]{3,2,1,0:T(8,128)(2,1)S(1)}, u32[]{:S(2)}, u32[]{:S(2)}) %collective-permute-start.20) | collective-permute-done | bytes 262176 | tf_op jit(solution)/shard_map/cond/branch_1_fun/ppermute | solution.py:118
  90.1 1.9 %collective-permute-done.21.far = bf16[8,2,32,512]{3,2,1,0:T(8,128)(2,1)S(1)} collective-permute-done((bf16[8,2,32,512]{3,2,1,0:T(8,128)(2,1)S(1)}, bf16[8,2,32,512]{3,2,1,0:T(8,128)(2,1)S(1)}, u32[]{:S(2)}, u32[]{:S(2)}) %collective-permute-start.21) | collective-permute-done | bytes 524320 | tf_op jit(solution)/shard_map/cond/branch_1_fun/ppermute | solution.py:112
  92.0 2.1 %branch_1_fun.15 = (bf16[256,512]{1,0:T(8,128)(2,1)S(1)}, bf16[512,512]{1,0:T(8,128)(2,1)S(1)}, bf16[512,512]{1,0:T(8,128)(2,1)S(1)}) custom-call(s32[8]{0:T(128)S(1)} %get-tuple-element.71.plan, bf16[8,2,32,512]{3,2,1,0:T(8,128)(2,1)S(1)} %constant_dynamic-update-slice_fusion.4.near, bf16[8,2,32,512]{3,2,1,0:T(8,128)(2,1)S(1)} %collective-permute-done.21.far, ...), custom_call_target="tpu_custom_call" | custom-call | flops 268435456 | bytes 1048576 | tf_op jit(solution)/shard_map/cond/branch_1_fun/pallas_call | solution.py:548
  94.6 4.9 %shard_map.47.gamma_in = bf16[2,2048,512]{2,1,0:T(8,128)(2,1)} custom-call(s32[8]{0:T(128)S(1)} %get-tuple-element.96.plan, bf16[8,1,32,512]{3,2,1,0:T(8,128)(2,1)} %get-tuple-element.112.near01, bf16[8,1,32,512]{3,2,1,0:T(8,128)(2,1)} %get-tuple-element.113.far01, bf16[512,512]{1,0:T(8,128)(2,1)S(1)} %get-tuple-element.114.amp0, ...), custom_call_target="tpu_custom_call" | custom-call | flops 3221225472 | bytes 1048576 | tf_op jit(solution)/shard_map/pallas_call | solution.py:564
  99.5 2.9 %collective-permute-done.25.back = bf16[256,512]{1,0:T(8,128)(2,1)S(1)} collective-permute-done((bf16[256,512]{1,0:T(8,128)(2,1)S(1)}, bf16[256,512]{1,0:T(8,128)(2,1)S(1)}, u32[]{:S(2)}, u32[]{:S(2)}) %collective-permute-start.25) | collective-permute-done | bytes 262176 | tf_op jit(solution)/shard_map/ppermute | solution.py:112
  (52 shorter events, 18.7 us)
Async XLA Ops:
  0.0 9.2 %copy-start.1 = (f32[4,512]{1,0:T(4,128)S(1)}, f32[4,512]{1,0:T(4,128)}, u32[]{:S(2)}) copy-start(f32[4,512]{1,0:T(4,128)} %param.12) | copy-start | bytes 24580
  0.0 9.3 %copy-start.2 = (f32[4]{0:T(128)S(1)}, f32[4]{0:T(128)}, u32[]{:S(2)}) copy-start(f32[4]{0:T(128)} %param.11) | copy-start | bytes 52
  3.7 37.7 %collective-permute-start.22 = (bf16[1536,512]{1,0:T(8,128)(2,1)}, bf16[1536,512]{1,0:T(8,128)(2,1)}, u32[]{:S(2)}, u32[]{:S(2)}) collective-permute-start(bf16[1536,512]{1,0:T(8,128)(2,1)} %get-tuple-element.97), channel_id=1, source_target_pairs={{0,16},{16,0},{1,17},{17,1},{2,18},{18,2},{3,19},{19,3},{4,20},{20... | collective-permute-start | bytes 4718600 | tf_op jit(solution)/shard_map/ppermute | solution.py:112
  9.3 16.6 %copy-start = (bf16[2,2048,512]{2,1,0:T(8,128)(2,1)S(1)}, bf16[2,2048,512]{2,1,0:T(8,128)(2,1)}, u32[]{:S(2)}) copy-start(bf16[2,2048,512]{2,1,0:T(8,128)(2,1)} %get-tuple-element.44.factors) | copy-start | bytes 12582916 | tf_op jit(solution)/shard_map/cond
  13.0 1.6 %collective-permute-start = (bf16[1,256,512]{2,1,0:T(8,128)(2,1)S(1)}, bf16[1,256,512]{2,1,0:T(8,128)(2,1)S(1)}, u32[]{:S(2)}, u32[]{:S(2)}) collective-permute-start(bf16[1,256,512]{2,1,0:T(8,128)(2,1)S(1)} %get-tuple-element.46), channel_id=1, source_target_pairs={{0,1},{1,0},{2,3},{3,2},{4,5},{5,4},{6,7},{7,6},{8,9},{9,8},{10,11... | collective-permute-start | bytes 786440 | tf_op jit(solution)/shard_map/cond/branch_1_fun/ppermute | solution.py:112
  15.2 5.6 %collective-permute-start.1 = (bf16[1,128,512]{2,1,0:T(8,128)(2,1)S(1)}, bf16[1,128,512]{2,1,0:T(8,128)(2,1)S(1)}, u32[]{:S(2)}, u32[]{:S(2)}) collective-permute-start(bf16[1,128,512]{2,1,0:T(8,128)(2,1)S(1)} %get-tuple-element.48), channel_id=1, source_target_pairs={{0,2},{1,3},{2,0},{3,1},{4,6},{5,7},{6,4},{7,5},{8,10},{9,11},{10,... | collective-permute-start | bytes 393224 | tf_op jit(solution)/shard_map/cond/branch_1_fun/ppermute | solution.py:118
  21.4 6.9 %collective-permute-start.2 = (bf16[1,32,512]{2,1,0:T(8,128)(2,1)S(1)}, bf16[1,32,512]{2,1,0:T(8,128)(2,1)S(1)}, u32[]{:S(2)}, u32[]{:S(2)}) collective-permute-start(bf16[1,32,512]{2,1,0:T(8,128)(2,1)S(1)} %get-tuple-element.50), channel_id=1, source_target_pairs={{0,8},{1,9},{2,10},{3,11},{4,12},{5,13},{6,14},{7,15},{8,0},{9,1},... | collective-permute-start | bytes 98312 | tf_op jit(solution)/shard_map/cond/branch_1_fun/ppermute | solution.py:118
  24.0 4.2 %collective-permute-start.3 = (bf16[1,32,512]{2,1,0:T(8,128)(2,1)S(1)}, bf16[1,32,512]{2,1,0:T(8,128)(2,1)S(1)}, u32[]{:S(2)}, u32[]{:S(2)}) collective-permute-start(bf16[1,32,512]{2,1,0:T(8,128)(2,1)S(1)} %get-tuple-element.51), channel_id=1, source_target_pairs={{0,4},{1,5},{2,6},{3,7},{4,0},{5,1},{6,2},{7,3},{8,12},{9,13},{10,... | collective-permute-start | bytes 98312 | tf_op jit(solution)/shard_map/cond/branch_1_fun/ppermute | solution.py:118
  25.6 5.7 %collective-permute-start.4 = (bf16[1,32,512]{2,1,0:T(8,128)(2,1)S(1)}, bf16[1,32,512]{2,1,0:T(8,128)(2,1)S(1)}, u32[]{:S(2)}, u32[]{:S(2)}) collective-permute-start(bf16[1,32,512]{2,1,0:T(8,128)(2,1)S(1)} %get-tuple-element.52), channel_id=1, source_target_pairs={{0,12},{1,13},{2,14},{3,15},{4,8},{5,9},{6,10},{7,11},{8,4},{9,5},... | collective-permute-start | bytes 98312 | tf_op jit(solution)/shard_map/cond/branch_1_fun/ppermute | solution.py:118
  31.3 5.8 %collective-permute-start.7 = (bf16[1,32,512]{2,1,0:T(8,128)(2,1)S(1)}, bf16[1,32,512]{2,1,0:T(8,128)(2,1)S(1)}, u32[]{:S(2)}, u32[]{:S(2)}) collective-permute-start(bf16[1,32,512]{2,1,0:T(8,128)(2,1)S(1)} %multiply_convert_fusion), channel_id=1, source_target_pairs={{0,12},{1,13},{2,14},{3,15},{4,8},{5,9},{6,10},{7,11},{8,4},{9,5},... | collective-permute-start | bytes 98312 | tf_op jit(solution)/shard_map/cond/branch_1_fun/ppermute | solution.py:118
  32.0 5.1 %collective-permute-start.6 = (bf16[1,32,512]{2,1,0:T(8,128)(2,1)S(1)}, bf16[1,32,512]{2,1,0:T(8,128)(2,1)S(1)}, u32[]{:S(2)}, u32[]{:S(2)}) collective-permute-start(bf16[1,32,512]{2,1,0:T(8,128)(2,1)S(1)} %multiply_convert_fusion), channel_id=1, source_target_pairs={{0,4},{1,5},{2,6},{3,7},{4,0},{5,1},{6,2},{7,3},{8,12},{9,13},{10,... | collective-permute-start | bytes 98312 | tf_op jit(solution)/shard_map/cond/branch_1_fun/ppermute | solution.py:118
  32.0 5.7 %collective-permute-start.5 = (bf16[1,32,512]{2,1,0:T(8,128)(2,1)S(1)}, bf16[1,32,512]{2,1,0:T(8,128)(2,1)S(1)}, u32[]{:S(2)}, u32[]{:S(2)}) collective-permute-start(bf16[1,32,512]{2,1,0:T(8,128)(2,1)S(1)} %multiply_convert_fusion), channel_id=1, source_target_pairs={{0,8},{1,9},{2,10},{3,11},{4,12},{5,13},{6,14},{7,15},{8,0},{9,1},... | collective-permute-start | bytes 98312 | tf_op jit(solution)/shard_map/cond/branch_1_fun/ppermute | solution.py:118
  41.4 27.9 %collective-permute-start.23 = (bf16[1152,512]{1,0:T(8,128)(2,1)S(1)}, bf16[1152,512]{1,0:T(8,128)(2,1)S(1)}, u32[]{:S(2)}, u32[]{:S(2)}) collective-permute-start(bf16[1152,512]{1,0:T(8,128)(2,1)S(1)} %get-tuple-element.105), channel_id=1, source_target_pairs={{0,16},{16,0},{1,17},{17,1},{2,18},{18,2},{3,19},{19,3},{4,20},{20... | collective-permute-start | bytes 3538952 | tf_op jit(solution)/shard_map/ppermute | solution.py:112
  46.5 2.0 %collective-permute-start.10 = (bf16[2,256,512]{2,1,0:T(8,128)(2,1)S(1)}, bf16[2,256,512]{2,1,0:T(8,128)(2,1)S(1)}, u32[]{:S(2)}, u32[]{:S(2)}) collective-permute-start(bf16[2,256,512]{2,1,0:T(8,128)(2,1)S(1)} %get-tuple-element.63), channel_id=1, source_target_pairs={{0,1},{1,0},{2,3},{3,2},{4,5},{5,4},{6,7},{7,6},{8,9},{9,8},{10,11... | collective-permute-start | bytes 1572872 | tf_op jit(solution)/shard_map/cond/branch_1_fun/ppermute | solution.py:112
  49.1 9.2 %collective-permute-start.11 = (bf16[2,128,512]{2,1,0:T(8,128)(2,1)S(1)}, bf16[2,128,512]{2,1,0:T(8,128)(2,1)S(1)}, u32[]{:S(2)}, u32[]{:S(2)}) collective-permute-start(bf16[2,128,512]{2,1,0:T(8,128)(2,1)S(1)} %get-tuple-element.65), channel_id=1, source_target_pairs={{0,2},{1,3},{2,0},{3,1},{4,6},{5,7},{6,4},{7,5},{8,10},{9,11},{10,... | collective-permute-start | bytes 786440 | tf_op jit(solution)/shard_map/cond/branch_1_fun/ppermute | solution.py:118
  50.7 12.7 %collective-permute-start.15 = (bf16[4,1,32,512]{3,2,1,0:T(8,128)(2,1)S(1)}, bf16[4,1,32,512]{3,2,1,0:T(8,128)(2,1)S(1)}, u32[]{:S(2)}, u32[]{:S(2)}) collective-permute-start(bf16[4,1,32,512]{3,2,1,0:T(8,128)(2,1)S(1)} %get-tuple-element.70), channel_id=1, source_target_pairs={{0,2},{1,3},{2,0},{3,1},{4,6},{5,7},{6,4},{7,5},{8,10},{9,11},{10,... | collective-permute-start | bytes 393224 | tf_op jit(solution)/shard_map/cond/branch_1_fun/ppermute | solution.py:118
  58.9 6.5 %collective-permute-start.12 = (bf16[2,32,512]{2,1,0:T(8,128)(2,1)S(1)}, bf16[2,32,512]{2,1,0:T(8,128)(2,1)S(1)}, u32[]{:S(2)}, u32[]{:S(2)}) collective-permute-start(bf16[2,32,512]{2,1,0:T(8,128)(2,1)S(1)} %get-tuple-element.67), channel_id=1, source_target_pairs={{0,8},{1,9},{2,10},{3,11},{4,12},{5,13},{6,14},{7,15},{8,0},{9,1},... | collective-permute-start | bytes 196616 | tf_op jit(solution)/shard_map/cond/branch_1_fun/ppermute | solution.py:118
  61.6 5.0 %collective-permute-start.13 = (bf16[2,32,512]{2,1,0:T(8,128)(2,1)S(1)}, bf16[2,32,512]{2,1,0:T(8,128)(2,1)S(1)}, u32[]{:S(2)}, u32[]{:S(2)}) collective-permute-start(bf16[2,32,512]{2,1,0:T(8,128)(2,1)S(1)} %get-tuple-element.68), channel_id=1, source_target_pairs={{0,4},{1,5},{2,6},{3,7},{4,0},{5,1},{6,2},{7,3},{8,12},{9,13},{10,... | collective-permute-start | bytes 196616 | tf_op jit(solution)/shard_map/cond/branch_1_fun/ppermute | solution.py:118
  63.2 6.1 %collective-permute-start.14 = (bf16[2,32,512]{2,1,0:T(8,128)(2,1)S(1)}, bf16[2,32,512]{2,1,0:T(8,128)(2,1)S(1)}, u32[]{:S(2)}, u32[]{:S(2)}) collective-permute-start(bf16[2,32,512]{2,1,0:T(8,128)(2,1)S(1)} %get-tuple-element.69), channel_id=1, source_target_pairs={{0,12},{1,13},{2,14},{3,15},{4,8},{5,9},{6,10},{7,11},{8,4},{9,5},... | collective-permute-start | bytes 196616 | tf_op jit(solution)/shard_map/cond/branch_1_fun/ppermute | solution.py:118
  64.1 5.2 %collective-permute-start.16 = (bf16[8,1,32,512]{3,2,1,0:T(8,128)(2,1)}, bf16[8,1,32,512]{3,2,1,0:T(8,128)(2,1)}, u32[]{:S(2)}, u32[]{:S(2)}) collective-permute-start(bf16[8,1,32,512]{3,2,1,0:T(8,128)(2,1)} %constant_dynamic-update-slice_fusion.2), channel_id=1, source_target_pairs={{0,1},{1,0},{2,3},{3,2},{4,5},{5,4},{6,7},{7,6},{8,9},{9,8},{10,11... | collective-permute-start | bytes 786440 | tf_op jit(solution)/shard_map/cond/branch_1_fun/ppermute | solution.py:112
  69.3 4.9 %collective-permute-start.24 = (bf16[2,32,512]{2,1,0:T(8,128)(2,1)S(1)}, bf16[2,32,512]{2,1,0:T(8,128)(2,1)S(1)}, u32[]{:S(2)}, u32[]{:S(2)}) collective-permute-start(bf16[2,32,512]{2,1,0:T(8,128)(2,1)S(1)} %convert_element_type.43), channel_id=1, source_target_pairs={{0,16},{16,0},{1,17},{17,1},{2,18},{18,2},{3,19},{19,3},{4,20},{20... | collective-permute-start | bytes 196616 | tf_op jit(solution)/shard_map/ppermute | solution.py:112
  74.3 20.4 %collective-permute-start.26 = (bf16[896,512]{1,0:T(8,128)(2,1)}, bf16[896,512]{1,0:T(8,128)(2,1)S(1)}, u32[]{:S(2)}, u32[]{:S(2)}) collective-permute-start(bf16[896,512]{1,0:T(8,128)(2,1)} %get-tuple-element.117), channel_id=1, source_target_pairs={{0,16},{16,0},{1,17},{17,1},{2,18},{18,2},{3,19},{19,3},{4,20},{20... | collective-permute-start | bytes 2752520 | tf_op jit(solution)/shard_map/ppermute | solution.py:112
  75.7 6.1 %collective-permute-start.19 = (bf16[2,32,512]{2,1,0:T(8,128)(2,1)S(1)}, bf16[2,32,512]{2,1,0:T(8,128)(2,1)S(1)}, u32[]{:S(2)}, u32[]{:S(2)}) collective-permute-start(bf16[2,32,512]{2,1,0:T(8,128)(2,1)S(1)} %get-tuple-element.72), channel_id=1, source_target_pairs={{0,12},{1,13},{2,14},{3,15},{4,8},{5,9},{6,10},{7,11},{8,4},{9,5},... | collective-permute-start | bytes 196616 | tf_op jit(solution)/shard_map/cond/branch_1_fun/ppermute | solution.py:118
  78.3 4.3 %collective-permute-start.18 = (bf16[2,32,512]{2,1,0:T(8,128)(2,1)S(1)}, bf16[2,32,512]{2,1,0:T(8,128)(2,1)S(1)}, u32[]{:S(2)}, u32[]{:S(2)}) collective-permute-start(bf16[2,32,512]{2,1,0:T(8,128)(2,1)S(1)} %get-tuple-element.72), channel_id=1, source_target_pairs={{0,4},{1,5},{2,6},{3,7},{4,0},{5,1},{6,2},{7,3},{8,12},{9,13},{10,... | collective-permute-start | bytes 196616 | tf_op jit(solution)/shard_map/cond/branch_1_fun/ppermute | solution.py:118
  78.3 5.2 %collective-permute-start.17 = (bf16[2,32,512]{2,1,0:T(8,128)(2,1)S(1)}, bf16[2,32,512]{2,1,0:T(8,128)(2,1)S(1)}, u32[]{:S(2)}, u32[]{:S(2)}) collective-permute-start(bf16[2,32,512]{2,1,0:T(8,128)(2,1)S(1)} %get-tuple-element.72), channel_id=1, source_target_pairs={{0,8},{1,9},{2,10},{3,11},{4,12},{5,13},{6,14},{7,15},{8,0},{9,1},... | collective-permute-start | bytes 196616 | tf_op jit(solution)/shard_map/cond/branch_1_fun/ppermute | solution.py:118
  83.5 6.4 %collective-permute-start.20 = (bf16[4,2,32,512]{3,2,1,0:T(8,128)(2,1)S(1)}, bf16[4,2,32,512]{3,2,1,0:T(8,128)(2,1)S(1)}, u32[]{:S(2)}, u32[]{:S(2)}) collective-permute-start(bf16[4,2,32,512]{3,2,1,0:T(8,128)(2,1)S(1)} %pad_maximum_fusion.1), channel_id=1, source_target_pairs={{0,2},{1,3},{2,0},{3,1},{4,6},{5,7},{6,4},{7,5},{8,10},{9,11},{10,... | collective-permute-start | bytes 786440 | tf_op jit(solution)/shard_map/cond/branch_1_fun/ppermute | solution.py:118
  90.0 2.0 %collective-permute-start.21 = (bf16[8,2,32,512]{3,2,1,0:T(8,128)(2,1)S(1)}, bf16[8,2,32,512]{3,2,1,0:T(8,128)(2,1)S(1)}, u32[]{:S(2)}, u32[]{:S(2)}) collective-permute-start(bf16[8,2,32,512]{3,2,1,0:T(8,128)(2,1)S(1)} %constant_dynamic-update-slice_fusion.4.near), channel_id=1, source_target_pairs={{0,1},{1,0},{2,3},{3,2},{4,5},{5,4},{6,7},{7,6},{8,9},{9,8},{10,11... | collective-permute-start | bytes 1572872 | tf_op jit(solution)/shard_map/cond/branch_1_fun/ppermute | solution.py:112
  94.1 8.4 %collective-permute-start.25 = (bf16[256,512]{1,0:T(8,128)(2,1)S(1)}, bf16[256,512]{1,0:T(8,128)(2,1)S(1)}, u32[]{:S(2)}, u32[]{:S(2)}) collective-permute-start(bf16[256,512]{1,0:T(8,128)(2,1)S(1)} %get-tuple-element.111), channel_id=1, source_target_pairs={{0,16},{16,0},{1,17},{17,1},{2,18},{18,2},{3,19},{19,3},{4,20},{20... | collective-permute-start | bytes 786440 | tf_op jit(solution)/shard_map/ppermute | solution.py:112

commit v2 on v1

--- a/solution.py
+++ b/solution.py
@@ -371,10 +371,14 @@
             at = slice(n * step, (n + 1) * step)
             first = right_t(own[1, at], own_amp[...]) + right_t(rows[at], amp0[...])
             out[0, at] = first.astype(out.dtype)
+            place = part(2 * n, 2)
+            results.append(pltpu.make_async_copy(out.at[0, place], gamma.at[0, place], outs.at[n]))
+            results[-1].start()
             second = right(own[0, at], own_amp[...]) + right_t(rows[at], amp1[...])
             out[1, at] = second.astype(out.dtype)
-            place = part(2 * n, 2)
-            results.append(pltpu.make_async_copy(out.at[:, place], gamma.at[:, place], outs.at[n]))
+            results.append(
+                pltpu.make_async_copy(out.at[1, place], gamma.at[1, place], outs.at[4 + n])
+            )
             results[-1].start()
         wait_all(results)
 
@@ -573,7 +577,7 @@
             pltpu.VMEM(factors.shape, dtype),
             pltpu.VMEM((width, width), dtype),
             dma((12,)),
-            dma((5,)),
+            dma((8,)),
         ],
         12,
         mebi=32,

time: 104 us -> 104 us (level)
  no operation moved by 1% of the time
where the time goes in v2:
time: 104 us
  waiting for transfers between devices  44.4 us (43%)
  starting transfers between devices  31.2 us (30%)
  Pallas kernels  23.8 us (23%)
  local copies, waits for them, and re-layouts  2.04 us (2%)
  between operations  1.95 us (2%)
    ppermute x16, waiting for transfers between devices, direct(): return lax.ppermute(value, 'aux', [(i, i ^ mask) for i in range(size)])  28.9 us
    ppermute x16, starting transfers between devices, direct(): return lax.ppermute(value, 'aux', [(i, i ^ mask) for i in range(size)])  23 us
    ppermute x9, waiting for transfers between devices, swap(): return lax.ppermute(value, axis, [(i, i ^ 1 << bit) for i in range(size)])  15.6 us
    ppermute x9, starting transfers between devices, swap(): return lax.ppermute(value, axis, [(i, i ^ 1 << bit) for i in range(size)])  8.26 us
    pallas_call x1, Pallas kernels, two_groups(): call(functools.partial(last_kernel, step), array(*factors.shape), [SMEM_S...  4.91 us
    pallas_call x1, Pallas kernels, own_chain(): call(functools.partial(own_kernel, step), halves(1), [SMEM_SPEC, HBM_SPEC...  3.69 us
    pallas_call x1, Pallas kernels, two_groups(): call(functools.partial(plan_kernel, tile_table.shape[0], bits, step), (ar...  3.66 us
    pallas_call x1, Pallas kernels, pair_chain(): call(functools.partial(pair_kernel, step), halves(2), [SMEM_SPEC, HBM_SPE...  3.34 us
  transfers between devices with their start and end apart: 25, of which 18 were waited for; matrix products, arithmetic and copies ran while one was open for 2% of the time, Pallas kernels for 18%

profile of v2, /device:TPU:0, one launch (start us, length us, event | category | flops | bytes accessed | tf_op | source)
XLA Modules:
  0.0 103.7 jit_solution(17913488644102828569)
XLA Ops:
  0.0 3.7 %shard_map.46 = (s32[8]{0:T(128)S(1)}, bf16[1536,512]{1,0:T(8,128)(2,1)}) custom-call(s32[4,3]{1,0:T(4,128)} %table.1, bf16[2,2048,512]{2,1,0:T(8,128)(2,1)} %factors.3), custom_call_target="tpu_custom_call" | custom-call | bytes 1048576 | tf_op jit(solution)/shard_map/pallas_call | solution.py:449
  3.7 3.0 %collective-permute-start.22 = (bf16[1536,512]{1,0:T(8,128)(2,1)}, bf16[1536,512]{1,0:T(8,128)(2,1)}, u32[]{:S(2)}, u32[]{:S(2)}) collective-permute-start(bf16[1536,512]{1,0:T(8,128)(2,1)} %get-tuple-element.97), channel_id=1, source_target_pairs={{0,16},{16,0},{1,17},{17,1},{2,18},{18,2},{3,19},{19,3},{4,20},{20... | collective-permute-start | bytes 4718600 | tf_op jit(solution)/shard_map/ppermute | solution.py:112
  9.3 28.4 %conditional.3 = (bf16[4,1,32,512]{3,2,1,0:T(8,128)(2,1)S(1)}, f32[2,32,512]{2,1,0:T(8,128)S(1)}, bf16[1152,512]{1,0:T(8,128)(2,1)S(1)}, bf16[896,512]{1,0:T(8,128)(2,1)}) conditional(s32[]{:T(128)} %bitcast.8, (s32[8]{0:T(128)S(1)}, f32[4]{0:T(128)S(1)}, f32[4,512]{1,0:T(4,128)S(1)}, bf16[2,2048,512]{2,1,0:T(8,128)(2,1)}) %tuple.51, ...), branch_computations={%region_0.0_spmd, %region_1.0_spmd} | conditional | flops 1074069504 | bytes 23855484 | solution.py:514
  9.3 3.7 %branch_1_fun.8 = (f32[1,256,512]{2,1,0:T(8,128)S(1)}, bf16[1,256,512]{2,1,0:T(8,128)(2,1)S(1)}) custom-call(s32[8]{0:T(128)S(1)} %get-tuple-element.43.plan, bf16[2,2048,512]{2,1,0:T(8,128)(2,1)} %get-tuple-element.44.factors), custom_call_target="tpu_custom_call" | custom-call | flops 1073741824 | bytes 1048576 | tf_op jit(solution)/shard_map/cond/branch_1_fun/pallas_call | solution.py:499
  15.2 1.6 %collective-permute-start.1 = (bf16[1,128,512]{2,1,0:T(8,128)(2,1)S(1)}, bf16[1,128,512]{2,1,0:T(8,128)(2,1)S(1)}, u32[]{:S(2)}, u32[]{:S(2)}) collective-permute-start(bf16[1,128,512]{2,1,0:T(8,128)(2,1)S(1)} %get-tuple-element.48), channel_id=1, source_target_pairs={{0,2},{1,3},{2,0},{3,1},{4,6},{5,7},{6,4},{7,5},{8,10},{9,11},{10,... | collective-permute-start | bytes 393224 | tf_op jit(solution)/shard_map/cond/branch_1_fun/ppermute | solution.py:118
  16.8 4.0 %collective-permute-done.1.came = bf16[1,128,512]{2,1,0:T(8,128)(2,1)S(1)} collective-permute-done((bf16[1,128,512]{2,1,0:T(8,128)(2,1)S(1)}, bf16[1,128,512]{2,1,0:T(8,128)(2,1)S(1)}, u32[]{:S(2)}, u32[]{:S(2)}) %collective-permute-start.1) | collective-permute-done | bytes 131104 | tf_op jit(solution)/shard_map/cond/branch_1_fun/ppermute | solution.py:118
  21.4 2.7 %collective-permute-start.2 = (bf16[1,32,512]{2,1,0:T(8,128)(2,1)S(1)}, bf16[1,32,512]{2,1,0:T(8,128)(2,1)S(1)}, u32[]{:S(2)}, u32[]{:S(2)}) collective-permute-start(bf16[1,32,512]{2,1,0:T(8,128)(2,1)S(1)} %get-tuple-element.50), channel_id=1, source_target_pairs={{0,8},{1,9},{2,10},{3,11},{4,12},{5,13},{6,14},{7,15},{8,0},{9,1},... | collective-permute-start | bytes 98312 | tf_op jit(solution)/shard_map/cond/branch_1_fun/ppermute | solution.py:118
  24.0 1.6 %collective-permute-start.3 = (bf16[1,32,512]{2,1,0:T(8,128)(2,1)S(1)}, bf16[1,32,512]{2,1,0:T(8,128)(2,1)S(1)}, u32[]{:S(2)}, u32[]{:S(2)}) collective-permute-start(bf16[1,32,512]{2,1,0:T(8,128)(2,1)S(1)} %get-tuple-element.51), channel_id=1, source_target_pairs={{0,4},{1,5},{2,6},{3,7},{4,0},{5,1},{6,2},{7,3},{8,12},{9,13},{10,... | collective-permute-start | bytes 98312 | tf_op jit(solution)/shard_map/cond/branch_1_fun/ppermute | solution.py:118
  25.8 2.4 %branch_1_fun.11 = (f32[1,32,512]{2,1,0:T(8,128)S(1)}, f32[2,32,512]{2,1,0:T(8,128)S(1)}, bf16[1152,512]{1,0:T(8,128)(2,1)S(1)}, bf16[896,512]{1,0:T(8,128)(2,1)}) custom-call(s32[8]{0:T(128)S(1)} %get-tuple-element.43.plan, f32[4]{0:T(128)S(1)} %get-tuple-element.53.occ, f32[4,512]{1,0:T(4,128)S(1)} %get-tuple-element.54.virt, bf16[2,2048,512]{2,1,0:T(8,128)(2,1)S(1)} %copy-done), custom_call_target="tpu_custom_call" | custom-call | bytes 1048576 | tf_op jit(solution)/shard_map/cond/branch_1_fun/pallas_call | solution.py:485
  28.3 3.0 %collective-permute-done.4 = bf16[1,32,512]{2,1,0:T(8,128)(2,1)S(1)} collective-permute-done((bf16[1,32,512]{2,1,0:T(8,128)(2,1)S(1)}, bf16[1,32,512]{2,1,0:T(8,128)(2,1)S(1)}, u32[]{:S(2)}, u32[]{:S(2)}) %collective-permute-start.4) | collective-permute-done | bytes 32800 | tf_op jit(solution)/shard_map/cond/branch_1_fun/ppermute | solution.py:118
  32.0 3.8 %collective-permute-start.5 = (bf16[1,32,512]{2,1,0:T(8,128)(2,1)S(1)}, bf16[1,32,512]{2,1,0:T(8,128)(2,1)S(1)}, u32[]{:S(2)}, u32[]{:S(2)}) collective-permute-start(bf16[1,32,512]{2,1,0:T(8,128)(2,1)S(1)} %multiply_convert_fusion), channel_id=1, source_target_pairs={{0,8},{1,9},{2,10},{3,11},{4,12},{5,13},{6,14},{7,15},{8,0},{9,1},... | collective-permute-start | bytes 98312 | tf_op jit(solution)/shard_map/cond/branch_1_fun/ppermute | solution.py:118
  37.7 3.7 %collective-permute-done.22.got1 = bf16[1536,512]{1,0:T(8,128)(2,1)} collective-permute-done((bf16[1536,512]{1,0:T(8,128)(2,1)}, bf16[1536,512]{1,0:T(8,128)(2,1)}, u32[]{:S(2)}, u32[]{:S(2)}) %collective-permute-start.22) | collective-permute-done | bytes 1572896 | tf_op jit(solution)/shard_map/ppermute | solution.py:112
  41.4 1.7 %collective-permute-start.23 = (bf16[1152,512]{1,0:T(8,128)(2,1)S(1)}, bf16[1152,512]{1,0:T(8,128)(2,1)S(1)}, u32[]{:S(2)}, u32[]{:S(2)}) collective-permute-start(bf16[1152,512]{1,0:T(8,128)(2,1)S(1)} %get-tuple-element.105), channel_id=1, source_target_pairs={{0,16},{16,0},{1,17},{17,1},{2,18},{18,2},{3,19},{19,3},{4,20},{20... | collective-permute-start | bytes 3538952 | tf_op jit(solution)/shard_map/ppermute | solution.py:112
  43.2 26.1 %conditional.4 = (f32[2,32,512]{2,1,0:T(8,128)S(1)}, bf16[8,1,32,512]{3,2,1,0:T(8,128)(2,1)}, bf16[8,1,32,512]{3,2,1,0:T(8,128)(2,1)}) conditional(s32[]{:T(128)} %convert_element_type.42, bf16[4,1,32,512]{3,2,1,0:T(8,128)(2,1)S(1)} %get-tuple-element.102, (s32[8]{0:T(128)S(1)}, bf16[2,2048,512]{2,1,0:T(8,128)(2,1)}, bf16[1536,512]{1,0:T(8,128)(2,1)}, ...), branch_computations={%region_2.0_spmd, %region_3.0_spmd} | conditional | flops 1342373888 | bytes 9634096 | solution.py:542
  43.2 3.3 %branch_1_fun.12 = (f32[2,256,512]{2,1,0:T(8,128)S(1)}, bf16[2,256,512]{2,1,0:T(8,128)(2,1)S(1)}) custom-call(s32[8]{0:T(128)S(1)} %get-tuple-element.59.plan, bf16[2,2048,512]{2,1,0:T(8,128)(2,1)} %get-tuple-element.60.factors, bf16[1536,512]{1,0:T(8,128)(2,1)} %get-tuple-element.61.got_hbm), custom_call_target="tpu_custom_call" | custom-call | flops 1342177280 | bytes 1048576 | tf_op jit(solution)/shard_map/cond/branch_1_fun/pallas_call | solution.py:522
  46.6 1.9 %collective-permute-done.10.came = bf16[2,256,512]{2,1,0:T(8,128)(2,1)S(1)} collective-permute-done((bf16[2,256,512]{2,1,0:T(8,128)(2,1)S(1)}, bf16[2,256,512]{2,1,0:T(8,128)(2,1)S(1)}, u32[]{:S(2)}, u32[]{:S(2)}) %collective-permute-start.10) | collective-permute-done | bytes 524320 | tf_op jit(solution)/shard_map/cond/branch_1_fun/ppermute | solution.py:112
  49.1 1.6 %collective-permute-start.11 = (bf16[2,128,512]{2,1,0:T(8,128)(2,1)S(1)}, bf16[2,128,512]{2,1,0:T(8,128)(2,1)S(1)}, u32[]{:S(2)}, u32[]{:S(2)}) collective-permute-start(bf16[2,128,512]{2,1,0:T(8,128)(2,1)S(1)} %get-tuple-element.65), channel_id=1, source_target_pairs={{0,2},{1,3},{2,0},{3,1},{4,6},{5,7},{6,4},{7,5},{8,10},{9,11},{10,... | collective-permute-start | bytes 786440 | tf_op jit(solution)/shard_map/cond/branch_1_fun/ppermute | solution.py:118
  51.9 6.5 %collective-permute-done.11.came = bf16[2,128,512]{2,1,0:T(8,128)(2,1)S(1)} collective-permute-done((bf16[2,128,512]{2,1,0:T(8,128)(2,1)S(1)}, bf16[2,128,512]{2,1,0:T(8,128)(2,1)S(1)}, u32[]{:S(2)}, u32[]{:S(2)}) %collective-permute-start.11) | collective-permute-done | bytes 262176 | tf_op jit(solution)/shard_map/cond/branch_1_fun/ppermute | solution.py:118
  58.9 2.7 %collective-permute-start.12 = (bf16[2,32,512]{2,1,0:T(8,128)(2,1)S(1)}, bf16[2,32,512]{2,1,0:T(8,128)(2,1)S(1)}, u32[]{:S(2)}, u32[]{:S(2)}) collective-permute-start(bf16[2,32,512]{2,1,0:T(8,128)(2,1)S(1)} %get-tuple-element.67), channel_id=1, source_target_pairs={{0,8},{1,9},{2,10},{3,11},{4,12},{5,13},{6,14},{7,15},{8,0},{9,1},... | collective-permute-start | bytes 196616 | tf_op jit(solution)/shard_map/cond/branch_1_fun/ppermute | solution.py:118
  61.6 1.6 %collective-permute-start.13 = (bf16[2,32,512]{2,1,0:T(8,128)(2,1)S(1)}, bf16[2,32,512]{2,1,0:T(8,128)(2,1)S(1)}, u32[]{:S(2)}, u32[]{:S(2)}) collective-permute-start(bf16[2,32,512]{2,1,0:T(8,128)(2,1)S(1)} %get-tuple-element.68), channel_id=1, source_target_pairs={{0,4},{1,5},{2,6},{3,7},{4,0},{5,1},{6,2},{7,3},{8,12},{9,13},{10,... | collective-permute-start | bytes 196616 | tf_op jit(solution)/shard_map/cond/branch_1_fun/ppermute | solution.py:118
  66.6 2.6 %collective-permute-done.14 = bf16[2,32,512]{2,1,0:T(8,128)(2,1)S(1)} collective-permute-done((bf16[2,32,512]{2,1,0:T(8,128)(2,1)S(1)}, bf16[2,32,512]{2,1,0:T(8,128)(2,1)S(1)}, u32[]{:S(2)}, u32[]{:S(2)}) %collective-permute-start.14) | collective-permute-done | bytes 65568 | tf_op jit(solution)/shard_map/cond/branch_1_fun/ppermute | solution.py:118
  70.6 3.6 %collective-permute-done.24 = bf16[2,32,512]{2,1,0:T(8,128)(2,1)S(1)} collective-permute-done((bf16[2,32,512]{2,1,0:T(8,128)(2,1)S(1)}, bf16[2,32,512]{2,1,0:T(8,128)(2,1)S(1)}, u32[]{:S(2)}, u32[]{:S(2)}) %collective-permute-start.24) | collective-permute-done | bytes 65568 | tf_op jit(solution)/shard_map/ppermute | solution.py:112
  75.7 18.4 %conditional.5 = ((bf16[256,512]{1,0:T(8,128)(2,1)S(1)}, bf16[512,512]{1,0:T(8,128)(2,1)S(1)}, bf16[512,512]{1,0:T(8,128)(2,1)S(1)})) conditional(s32[]{:T(128)} %convert_element_type.42, () %tuple.34, (bf16[2,32,512]{2,1,0:T(8,128)(2,1)S(1)}, s32[8]{0:T(128)S(1)}, bf16[2,2048,512]{2,1,0:T(8,128)(2,1)}) %tuple.38), branch_computations={%region_4.0_spmd, %region_5.0_spmd} | conditional | flops 268828672 | bytes 6553808 | solution.py:565
  75.7 2.6 %collective-permute-start.19 = (bf16[2,32,512]{2,1,0:T(8,128)(2,1)S(1)}, bf16[2,32,512]{2,1,0:T(8,128)(2,1)S(1)}, u32[]{:S(2)}, u32[]{:S(2)}) collective-permute-start(bf16[2,32,512]{2,1,0:T(8,128)(2,1)S(1)} %get-tuple-element.72), channel_id=1, source_target_pairs={{0,12},{1,13},{2,14},{3,15},{4,8},{5,9},{6,10},{7,11},{8,4},{9,5},... | collective-permute-start | bytes 196616 | tf_op jit(solution)/shard_map/cond/branch_1_fun/ppermute | solution.py:118
  78.3 1.8 %collective-permute-start.17 = (bf16[2,32,512]{2,1,0:T(8,128)(2,1)S(1)}, bf16[2,32,512]{2,1,0:T(8,128)(2,1)S(1)}, u32[]{:S(2)}, u32[]{:S(2)}) collective-permute-start(bf16[2,32,512]{2,1,0:T(8,128)(2,1)S(1)} %get-tuple-element.72), channel_id=1, source_target_pairs={{0,8},{1,9},{2,10},{3,11},{4,12},{5,13},{6,14},{7,15},{8,0},{9,1},... | collective-permute-start | bytes 196616 | tf_op jit(solution)/shard_map/cond/branch_1_fun/ppermute | solution.py:118
  80.1 1.7 %collective-permute-done.19 = bf16[2,32,512]{2,1,0:T(8,128)(2,1)S(1)} collective-permute-done((bf16[2,32,512]{2,1,0:T(8,128)(2,1)S(1)}, bf16[2,32,512]{2,1,0:T(8,128)(2,1)S(1)}, u32[]{:S(2)}, u32[]{:S(2)}) %collective-permute-start.19) | collective-permute-done | bytes 65568 | tf_op jit(solution)/shard_map/cond/branch_1_fun/ppermute | solution.py:118
  83.5 1.6 %collective-permute-start.20 = (bf16[4,2,32,512]{3,2,1,0:T(8,128)(2,1)S(1)}, bf16[4,2,32,512]{3,2,1,0:T(8,128)(2,1)S(1)}, u32[]{:S(2)}, u32[]{:S(2)}) collective-permute-start(bf16[4,2,32,512]{3,2,1,0:T(8,128)(2,1)S(1)} %pad_maximum_fusion.1), channel_id=1, source_target_pairs={{0,2},{1,3},{2,0},{3,1},{4,6},{5,7},{6,4},{7,5},{8,10},{9,11},{10,... | collective-permute-start | bytes 786440 | tf_op jit(solution)/shard_map/cond/branch_1_fun/ppermute | solution.py:118
  85.1 4.9 %collective-permute-done.20 = bf16[4,2,32,512]{3,2,1,0:T(8,128)(2,1)S(1)} collective-permute-done((bf16[4,2,32,512]{3,2,1,0:T(8,128)(2,1)S(1)}, bf16[4,2,32,512]{3,2,1,0:T(8,128)(2,1)S(1)}, u32[]{:S(2)}, u32[]{:S(2)}) %collective-permute-start.20) | collective-permute-done | bytes 262176 | tf_op jit(solution)/shard_map/cond/branch_1_fun/ppermute | solution.py:118
  90.1 1.9 %collective-permute-done.21.far = bf16[8,2,32,512]{3,2,1,0:T(8,128)(2,1)S(1)} collective-permute-done((bf16[8,2,32,512]{3,2,1,0:T(8,128)(2,1)S(1)}, bf16[8,2,32,512]{3,2,1,0:T(8,128)(2,1)S(1)}, u32[]{:S(2)}, u32[]{:S(2)}) %collective-permute-start.21) | collective-permute-done | bytes 524320 | tf_op jit(solution)/shard_map/cond/branch_1_fun/ppermute | solution.py:112
  92.0 2.1 %branch_1_fun.15 = (bf16[256,512]{1,0:T(8,128)(2,1)S(1)}, bf16[512,512]{1,0:T(8,128)(2,1)S(1)}, bf16[512,512]{1,0:T(8,128)(2,1)S(1)}) custom-call(s32[8]{0:T(128)S(1)} %get-tuple-element.71.plan, bf16[8,2,32,512]{3,2,1,0:T(8,128)(2,1)S(1)} %constant_dynamic-update-slice_fusion.4.near, bf16[8,2,32,512]{3,2,1,0:T(8,128)(2,1)S(1)} %collective-permute-done.21.far, ...), custom_call_target="tpu_custom_call" | custom-call | flops 268435456 | bytes 1048576 | tf_op jit(solution)/shard_map/cond/branch_1_fun/pallas_call | solution.py:552
  94.6 4.9 %shard_map.47.gamma_in = bf16[2,2048,512]{2,1,0:T(8,128)(2,1)} custom-call(s32[8]{0:T(128)S(1)} %get-tuple-element.96.plan, bf16[8,1,32,512]{3,2,1,0:T(8,128)(2,1)} %get-tuple-element.112.near01, bf16[8,1,32,512]{3,2,1,0:T(8,128)(2,1)} %get-tuple-element.113.far01, bf16[512,512]{1,0:T(8,128)(2,1)S(1)} %get-tuple-element.114.amp0, ...), custom_call_target="tpu_custom_call" | custom-call | flops 3221225472 | bytes 1048576 | tf_op jit(solution)/shard_map/pallas_call | solution.py:568
  99.6 2.9 %collective-permute-done.25.back = bf16[256,512]{1,0:T(8,128)(2,1)S(1)} collective-permute-done((bf16[256,512]{1,0:T(8,128)(2,1)S(1)}, bf16[256,512]{1,0:T(8,128)(2,1)S(1)}, u32[]{:S(2)}, u32[]{:S(2)}) %collective-permute-start.25) | collective-permute-done | bytes 262176 | tf_op jit(solution)/shard_map/ppermute | solution.py:112
  (52 shorter events, 18.7 us)
Async XLA Ops:
  0.0 9.2 %copy-start.1 = (f32[4,512]{1,0:T(4,128)S(1)}, f32[4,512]{1,0:T(4,128)}, u32[]{:S(2)}) copy-start(f32[4,512]{1,0:T(4,128)} %param.12) | copy-start | bytes 24580
  0.0 9.3 %copy-start.2 = (f32[4]{0:T(128)S(1)}, f32[4]{0:T(128)}, u32[]{:S(2)}) copy-start(f32[4]{0:T(128)} %param.11) | copy-start | bytes 52
  3.7 37.7 %collective-permute-start.22 = (bf16[1536,512]{1,0:T(8,128)(2,1)}, bf16[1536,512]{1,0:T(8,128)(2,1)}, u32[]{:S(2)}, u32[]{:S(2)}) collective-permute-start(bf16[1536,512]{1,0:T(8,128)(2,1)} %get-tuple-element.97), channel_id=1, source_target_pairs={{0,16},{16,0},{1,17},{17,1},{2,18},{18,2},{3,19},{19,3},{4,20},{20... | collective-permute-start | bytes 4718600 | tf_op jit(solution)/shard_map/ppermute | solution.py:112
  9.3 16.6 %copy-start = (bf16[2,2048,512]{2,1,0:T(8,128)(2,1)S(1)}, bf16[2,2048,512]{2,1,0:T(8,128)(2,1)}, u32[]{:S(2)}) copy-start(bf16[2,2048,512]{2,1,0:T(8,128)(2,1)} %get-tuple-element.44.factors) | copy-start | bytes 12582916 | tf_op jit(solution)/shard_map/cond
  13.0 1.6 %collective-permute-start = (bf16[1,256,512]{2,1,0:T(8,128)(2,1)S(1)}, bf16[1,256,512]{2,1,0:T(8,128)(2,1)S(1)}, u32[]{:S(2)}, u32[]{:S(2)}) collective-permute-start(bf16[1,256,512]{2,1,0:T(8,128)(2,1)S(1)} %get-tuple-element.46), channel_id=1, source_target_pairs={{0,1},{1,0},{2,3},{3,2},{4,5},{5,4},{6,7},{7,6},{8,9},{9,8},{10,11... | collective-permute-start | bytes 786440 | tf_op jit(solution)/shard_map/cond/branch_1_fun/ppermute | solution.py:112
  15.2 5.6 %collective-permute-start.1 = (bf16[1,128,512]{2,1,0:T(8,128)(2,1)S(1)}, bf16[1,128,512]{2,1,0:T(8,128)(2,1)S(1)}, u32[]{:S(2)}, u32[]{:S(2)}) collective-permute-start(bf16[1,128,512]{2,1,0:T(8,128)(2,1)S(1)} %get-tuple-element.48), channel_id=1, source_target_pairs={{0,2},{1,3},{2,0},{3,1},{4,6},{5,7},{6,4},{7,5},{8,10},{9,11},{10,... | collective-permute-start | bytes 393224 | tf_op jit(solution)/shard_map/cond/branch_1_fun/ppermute | solution.py:118
  21.4 6.9 %collective-permute-start.2 = (bf16[1,32,512]{2,1,0:T(8,128)(2,1)S(1)}, bf16[1,32,512]{2,1,0:T(8,128)(2,1)S(1)}, u32[]{:S(2)}, u32[]{:S(2)}) collective-permute-start(bf16[1,32,512]{2,1,0:T(8,128)(2,1)S(1)} %get-tuple-element.50), channel_id=1, source_target_pairs={{0,8},{1,9},{2,10},{3,11},{4,12},{5,13},{6,14},{7,15},{8,0},{9,1},... | collective-permute-start | bytes 98312 | tf_op jit(solution)/shard_map/cond/branch_1_fun/ppermute | solution.py:118
  24.0 4.2 %collective-permute-start.3 = (bf16[1,32,512]{2,1,0:T(8,128)(2,1)S(1)}, bf16[1,32,512]{2,1,0:T(8,128)(2,1)S(1)}, u32[]{:S(2)}, u32[]{:S(2)}) collective-permute-start(bf16[1,32,512]{2,1,0:T(8,128)(2,1)S(1)} %get-tuple-element.51), channel_id=1, source_target_pairs={{0,4},{1,5},{2,6},{3,7},{4,0},{5,1},{6,2},{7,3},{8,12},{9,13},{10,... | collective-permute-start | bytes 98312 | tf_op jit(solution)/shard_map/cond/branch_1_fun/ppermute | solution.py:118
  25.6 5.7 %collective-permute-start.4 = (bf16[1,32,512]{2,1,0:T(8,128)(2,1)S(1)}, bf16[1,32,512]{2,1,0:T(8,128)(2,1)S(1)}, u32[]{:S(2)}, u32[]{:S(2)}) collective-permute-start(bf16[1,32,512]{2,1,0:T(8,128)(2,1)S(1)} %get-tuple-element.52), channel_id=1, source_target_pairs={{0,12},{1,13},{2,14},{3,15},{4,8},{5,9},{6,10},{7,11},{8,4},{9,5},... | collective-permute-start | bytes 98312 | tf_op jit(solution)/shard_map/cond/branch_1_fun/ppermute | solution.py:118
  31.3 5.8 %collective-permute-start.7 = (bf16[1,32,512]{2,1,0:T(8,128)(2,1)S(1)}, bf16[1,32,512]{2,1,0:T(8,128)(2,1)S(1)}, u32[]{:S(2)}, u32[]{:S(2)}) collective-permute-start(bf16[1,32,512]{2,1,0:T(8,128)(2,1)S(1)} %multiply_convert_fusion), channel_id=1, source_target_pairs={{0,12},{1,13},{2,14},{3,15},{4,8},{5,9},{6,10},{7,11},{8,4},{9,5},... | collective-permute-start | bytes 98312 | tf_op jit(solution)/shard_map/cond/branch_1_fun/ppermute | solution.py:118
  32.0 5.1 %collective-permute-start.6 = (bf16[1,32,512]{2,1,0:T(8,128)(2,1)S(1)}, bf16[1,32,512]{2,1,0:T(8,128)(2,1)S(1)}, u32[]{:S(2)}, u32[]{:S(2)}) collective-permute-start(bf16[1,32,512]{2,1,0:T(8,128)(2,1)S(1)} %multiply_convert_fusion), channel_id=1, source_target_pairs={{0,4},{1,5},{2,6},{3,7},{4,0},{5,1},{6,2},{7,3},{8,12},{9,13},{10,... | collective-permute-start | bytes 98312 | tf_op jit(solution)/shard_map/cond/branch_1_fun/ppermute | solution.py:118
  32.0 5.7 %collective-permute-start.5 = (bf16[1,32,512]{2,1,0:T(8,128)(2,1)S(1)}, bf16[1,32,512]{2,1,0:T(8,128)(2,1)S(1)}, u32[]{:S(2)}, u32[]{:S(2)}) collective-permute-start(bf16[1,32,512]{2,1,0:T(8,128)(2,1)S(1)} %multiply_convert_fusion), channel_id=1, source_target_pairs={{0,8},{1,9},{2,10},{3,11},{4,12},{5,13},{6,14},{7,15},{8,0},{9,1},... | collective-permute-start | bytes 98312 | tf_op jit(solution)/shard_map/cond/branch_1_fun/ppermute | solution.py:118
  41.4 27.9 %collective-permute-start.23 = (bf16[1152,512]{1,0:T(8,128)(2,1)S(1)}, bf16[1152,512]{1,0:T(8,128)(2,1)S(1)}, u32[]{:S(2)}, u32[]{:S(2)}) collective-permute-start(bf16[1152,512]{1,0:T(8,128)(2,1)S(1)} %get-tuple-element.105), channel_id=1, source_target_pairs={{0,16},{16,0},{1,17},{17,1},{2,18},{18,2},{3,19},{19,3},{4,20},{20... | collective-permute-start | bytes 3538952 | tf_op jit(solution)/shard_map/ppermute | solution.py:112
  46.5 2.0 %collective-permute-start.10 = (bf16[2,256,512]{2,1,0:T(8,128)(2,1)S(1)}, bf16[2,256,512]{2,1,0:T(8,128)(2,1)S(1)}, u32[]{:S(2)}, u32[]{:S(2)}) collective-permute-start(bf16[2,256,512]{2,1,0:T(8,128)(2,1)S(1)} %get-tuple-element.63), channel_id=1, source_target_pairs={{0,1},{1,0},{2,3},{3,2},{4,5},{5,4},{6,7},{7,6},{8,9},{9,8},{10,11... | collective-permute-start | bytes 1572872 | tf_op jit(solution)/shard_map/cond/branch_1_fun/ppermute | solution.py:112
  49.1 9.2 %collective-permute-start.11 = (bf16[2,128,512]{2,1,0:T(8,128)(2,1)S(1)}, bf16[2,128,512]{2,1,0:T(8,128)(2,1)S(1)}, u32[]{:S(2)}, u32[]{:S(2)}) collective-permute-start(bf16[2,128,512]{2,1,0:T(8,128)(2,1)S(1)} %get-tuple-element.65), channel_id=1, source_target_pairs={{0,2},{1,3},{2,0},{3,1},{4,6},{5,7},{6,4},{7,5},{8,10},{9,11},{10,... | collective-permute-start | bytes 786440 | tf_op jit(solution)/shard_map/cond/branch_1_fun/ppermute | solution.py:118
  50.7 12.7 %collective-permute-start.15 = (bf16[4,1,32,512]{3,2,1,0:T(8,128)(2,1)S(1)}, bf16[4,1,32,512]{3,2,1,0:T(8,128)(2,1)S(1)}, u32[]{:S(2)}, u32[]{:S(2)}) collective-permute-start(bf16[4,1,32,512]{3,2,1,0:T(8,128)(2,1)S(1)} %get-tuple-element.70), channel_id=1, source_target_pairs={{0,2},{1,3},{2,0},{3,1},{4,6},{5,7},{6,4},{7,5},{8,10},{9,11},{10,... | collective-permute-start | bytes 393224 | tf_op jit(solution)/shard_map/cond/branch_1_fun/ppermute | solution.py:118
  58.9 6.5 %collective-permute-start.12 = (bf16[2,32,512]{2,1,0:T(8,128)(2,1)S(1)}, bf16[2,32,512]{2,1,0:T(8,128)(2,1)S(1)}, u32[]{:S(2)}, u32[]{:S(2)}) collective-permute-start(bf16[2,32,512]{2,1,0:T(8,128)(2,1)S(1)} %get-tuple-element.67), channel_id=1, source_target_pairs={{0,8},{1,9},{2,10},{3,11},{4,12},{5,13},{6,14},{7,15},{8,0},{9,1},... | collective-permute-start | bytes 196616 | tf_op jit(solution)/shard_map/cond/branch_1_fun/ppermute | solution.py:118
  61.6 5.0 %collective-permute-start.13 = (bf16[2,32,512]{2,1,0:T(8,128)(2,1)S(1)}, bf16[2,32,512]{2,1,0:T(8,128)(2,1)S(1)}, u32[]{:S(2)}, u32[]{:S(2)}) collective-permute-start(bf16[2,32,512]{2,1,0:T(8,128)(2,1)S(1)} %get-tuple-element.68), channel_id=1, source_target_pairs={{0,4},{1,5},{2,6},{3,7},{4,0},{5,1},{6,2},{7,3},{8,12},{9,13},{10,... | collective-permute-start | bytes 196616 | tf_op jit(solution)/shard_map/cond/branch_1_fun/ppermute | solution.py:118
  63.2 6.1 %collective-permute-start.14 = (bf16[2,32,512]{2,1,0:T(8,128)(2,1)S(1)}, bf16[2,32,512]{2,1,0:T(8,128)(2,1)S(1)}, u32[]{:S(2)}, u32[]{:S(2)}) collective-permute-start(bf16[2,32,512]{2,1,0:T(8,128)(2,1)S(1)} %get-tuple-element.69), channel_id=1, source_target_pairs={{0,12},{1,13},{2,14},{3,15},{4,8},{5,9},{6,10},{7,11},{8,4},{9,5},... | collective-permute-start | bytes 196616 | tf_op jit(solution)/shard_map/cond/branch_1_fun/ppermute | solution.py:118
  64.1 5.2 %collective-permute-start.16 = (bf16[8,1,32,512]{3,2,1,0:T(8,128)(2,1)}, bf16[8,1,32,512]{3,2,1,0:T(8,128)(2,1)}, u32[]{:S(2)}, u32[]{:S(2)}) collective-permute-start(bf16[8,1,32,512]{3,2,1,0:T(8,128)(2,1)} %constant_dynamic-update-slice_fusion.2), channel_id=1, source_target_pairs={{0,1},{1,0},{2,3},{3,2},{4,5},{5,4},{6,7},{7,6},{8,9},{9,8},{10,11... | collective-permute-start | bytes 786440 | tf_op jit(solution)/shard_map/cond/branch_1_fun/ppermute | solution.py:112
  69.3 4.9 %collective-permute-start.24 = (bf16[2,32,512]{2,1,0:T(8,128)(2,1)S(1)}, bf16[2,32,512]{2,1,0:T(8,128)(2,1)S(1)}, u32[]{:S(2)}, u32[]{:S(2)}) collective-permute-start(bf16[2,32,512]{2,1,0:T(8,128)(2,1)S(1)} %convert_element_type.43), channel_id=1, source_target_pairs={{0,16},{16,0},{1,17},{17,1},{2,18},{18,2},{3,19},{19,3},{4,20},{20... | collective-permute-start | bytes 196616 | tf_op jit(solution)/shard_map/ppermute | solution.py:112
  74.3 20.4 %collective-permute-start.26 = (bf16[896,512]{1,0:T(8,128)(2,1)}, bf16[896,512]{1,0:T(8,128)(2,1)S(1)}, u32[]{:S(2)}, u32[]{:S(2)}) collective-permute-start(bf16[896,512]{1,0:T(8,128)(2,1)} %get-tuple-element.117), channel_id=1, source_target_pairs={{0,16},{16,0},{1,17},{17,1},{2,18},{18,2},{3,19},{19,3},{4,20},{20... | collective-permute-start | bytes 2752520 | tf_op jit(solution)/shard_map/ppermute | solution.py:112
  75.7 6.1 %collective-permute-start.19 = (bf16[2,32,512]{2,1,0:T(8,128)(2,1)S(1)}, bf16[2,32,512]{2,1,0:T(8,128)(2,1)S(1)}, u32[]{:S(2)}, u32[]{:S(2)}) collective-permute-start(bf16[2,32,512]{2,1,0:T(8,128)(2,1)S(1)} %get-tuple-element.72), channel_id=1, source_target_pairs={{0,12},{1,13},{2,14},{3,15},{4,8},{5,9},{6,10},{7,11},{8,4},{9,5},... | collective-permute-start | bytes 196616 | tf_op jit(solution)/shard_map/cond/branch_1_fun/ppermute | solution.py:118
  78.3 4.3 %collective-permute-start.18 = (bf16[2,32,512]{2,1,0:T(8,128)(2,1)S(1)}, bf16[2,32,512]{2,1,0:T(8,128)(2,1)S(1)}, u32[]{:S(2)}, u32[]{:S(2)}) collective-permute-start(bf16[2,32,512]{2,1,0:T(8,128)(2,1)S(1)} %get-tuple-element.72), channel_id=1, source_target_pairs={{0,4},{1,5},{2,6},{3,7},{4,0},{5,1},{6,2},{7,3},{8,12},{9,13},{10,... | collective-permute-start | bytes 196616 | tf_op jit(solution)/shard_map/cond/branch_1_fun/ppermute | solution.py:118
  78.3 5.2 %collective-permute-start.17 = (bf16[2,32,512]{2,1,0:T(8,128)(2,1)S(1)}, bf16[2,32,512]{2,1,0:T(8,128)(2,1)S(1)}, u32[]{:S(2)}, u32[]{:S(2)}) collective-permute-start(bf16[2,32,512]{2,1,0:T(8,128)(2,1)S(1)} %get-tuple-element.72), channel_id=1, source_target_pairs={{0,8},{1,9},{2,10},{3,11},{4,12},{5,13},{6,14},{7,15},{8,0},{9,1},... | collective-permute-start | bytes 196616 | tf_op jit(solution)/shard_map/cond/branch_1_fun/ppermute | solution.py:118
  83.5 6.4 %collective-permute-start.20 = (bf16[4,2,32,512]{3,2,1,0:T(8,128)(2,1)S(1)}, bf16[4,2,32,512]{3,2,1,0:T(8,128)(2,1)S(1)}, u32[]{:S(2)}, u32[]{:S(2)}) collective-permute-start(bf16[4,2,32,512]{3,2,1,0:T(8,128)(2,1)S(1)} %pad_maximum_fusion.1), channel_id=1, source_target_pairs={{0,2},{1,3},{2,0},{3,1},{4,6},{5,7},{6,4},{7,5},{8,10},{9,11},{10,... | collective-permute-start | bytes 786440 | tf_op jit(solution)/shard_map/cond/branch_1_fun/ppermute | solution.py:118
  90.0 2.0 %collective-permute-start.21 = (bf16[8,2,32,512]{3,2,1,0:T(8,128)(2,1)S(1)}, bf16[8,2,32,512]{3,2,1,0:T(8,128)(2,1)S(1)}, u32[]{:S(2)}, u32[]{:S(2)}) collective-permute-start(bf16[8,2,32,512]{3,2,1,0:T(8,128)(2,1)S(1)} %constant_dynamic-update-slice_fusion.4.near), channel_id=1, source_target_pairs={{0,1},{1,0},{2,3},{3,2},{4,5},{5,4},{6,7},{7,6},{8,9},{9,8},{10,11... | collective-permute-start | bytes 1572872 | tf_op jit(solution)/shard_map/cond/branch_1_fun/ppermute | solution.py:112
  94.1 8.4 %collective-permute-start.25 = (bf16[256,512]{1,0:T(8,128)(2,1)S(1)}, bf16[256,512]{1,0:T(8,128)(2,1)S(1)}, u32[]{:S(2)}, u32[]{:S(2)}) collective-permute-start(bf16[256,512]{1,0:T(8,128)(2,1)S(1)} %get-tuple-element.111), channel_id=1, source_target_pairs={{0,16},{16,0},{1,17},{17,1},{2,18},{18,2},{3,19},{19,3},{4,20},{20... | collective-permute-start | bytes 786440 | tf_op jit(solution)/shard_map/ppermute | solution.py:112
